TPU v7x, 32 devices: a whole 2x2x4 slice. The times are simulated.
32 devices in a mesh: ctx: 8 (over z, x), head: 4 (over y, core).
Axes of the slice: x: 2, y: 2, z: 4, core: 2. Of those that a mesh axis runs over, the one named last changes fastest.
Arguments:
- queries: bfloat16 [2048, 4096], P('ctx', 'head'), may hold values from -64 to 64
- key_vectors: bfloat16 [2048, 1024], P('ctx', 'head'), may hold values from -4.5 to 4.5
- value_vectors: bfloat16 [2048, 1024], P('ctx', 'head'), may hold values from -6 to 6
- out_weight: bfloat16 [4096, 4096], P('head'), may hold values from -0.09375 to 0.09375
- offsets: int32 [5], replicated, may hold values from 0 to 2048, as said below
Outputs:
- projected: bfloat16 [4096, 2048], P('head', 'ctx')
Inputs may be any that keep to these rules, and one draw needn't show every extreme that they name: offsets[0] = 0 and offsets[4] = 2048; offsets rise strictly; every document has 1 to 1024 tokens and one has exactly 1024.
All inputs are finite; a program needn't handle non-finite values.
Results may differ from a plain program's by a relative error of at most 0.014.
Values may be sent and summed in bfloat16 or wider, within the bound.
No kernel may reach another device: no remote copies, remote signals or barrier semaphores. Data moves between devices by JAX's collectives and lax.ppermute only.
A program may use at most 64 MiB of HBM per device.

v0:
```python
import jax
import jax.numpy as jnp
from jax import lax
from jax.experimental import pallas as pl
from jax.experimental.pallas import tpu as pltpu
from jax.sharding import PartitionSpec as P

HEAD_DIM = 128
REACH = 15
LOG2E = 1.4426950408889634
masked_score = -1e30
PARTS = 2
VMEM_LIMIT = 20 * 1024 * 1024

vmem = pl.BlockSpec(memory_space=pltpu.VMEM)
smem = pl.BlockSpec(memory_space=pltpu.SMEM)
hbm = pl.BlockSpec(memory_space=pltpu.HBM)


def in_hbm(array):
    return pltpu.with_memory_space_constraint(array, pltpu.HBM)


def in_vmem(arrays):
    return [pltpu.with_memory_space_constraint(a, pltpu.VMEM) for a in arrays]


def params():
    return pltpu.CompilerParams(vmem_limit_bytes=VMEM_LIMIT)


def document_starts(offsets, first, rows):
    positions = first + lax.broadcasted_iota(jnp.int32, (1, rows), 1)
    starts = jnp.zeros((1, rows), jnp.int32)
    for i in range(1, offsets.shape[0] - 1):
        starts = jnp.where(positions >= offsets[i], offsets[i], starts)
    return starts


def scores_of(keys, query):
    return lax.dot_general(keys, query, (((1,), (1,)), ((), ())), preferred_element_type=jnp.float32)


def visible_keys(starts, key_start, rows, first):
    key_pos = key_start + lax.broadcasted_iota(jnp.int32, (rows, 1), 0)
    visible = key_pos >= starts
    if first is not None:
        visible = visible & (key_pos <= first + lax.broadcasted_iota(jnp.int32, (1, rows), 1))
    return visible


def score_block(q_ref, k_ref, visible, before):
    factor = HEAD_DIM ** -0.5 * LOG2E
    heads = q_ref.shape[1] // HEAD_DIM
    each = heads // (k_ref.shape[1] // HEAD_DIM)
    groups = [h // each for h in range(heads)]
    scores = [
        scores_of(k_ref[:, g * HEAD_DIM : (g + 1) * HEAD_DIM], q_ref[:, h * HEAD_DIM : (h + 1) * HEAD_DIM])
        for h, g in enumerate(groups)
    ]
    scores = [jnp.where(visible, s, masked_score) for s in scores]
    tops = [jnp.max(s, axis=0, keepdims=True) for s in scores]
    if before is not None:
        olds = [before[0][h : h + 1, :] for h in range(heads)]
        tops = [jnp.maximum(old, top) for old, top in zip(olds, tops)]
    weights = [jnp.exp2((s - top) * factor) for s, top in zip(scores, tops)]
    totals = [jnp.sum(w, axis=0, keepdims=True) for w in weights]
    weights = [w.astype(jnp.bfloat16) for w in weights]
    if before is None:
        return tops, totals, weights, None
    alphas = [jnp.exp2((old - top) * factor) for old, top in zip(olds, tops)]
    totals = [before[1][h : h + 1, :] * alphas[h] + totals[h] for h in range(heads)]
    return tops, totals, weights, alphas


def value_block(v_ref, weights, alphas, acc_ref):
    groups = v_ref.shape[1] // HEAD_DIM
    each = len(weights) // groups
    values = [v_ref[:, g * HEAD_DIM : (g + 1) * HEAD_DIM].T for g in range(groups)]
    sums = [jnp.dot(values[h // each], w, preferred_element_type=jnp.float32) for h, w in enumerate(weights)]
    if alphas is None:
        return sums
    return [acc_ref[h] * alphas[h] + s for h, s in enumerate(sums)]


def store_rows(ref, rows):
    for h, row in enumerate(rows):
        ref[h : h + 1, :] = row


def state_shapes(heads, rows):
    return [
        jax.ShapeDtypeStruct((heads, rows), jnp.float32),
        jax.ShapeDtypeStruct((heads, rows), jnp.float32),
        jax.ShapeDtypeStruct((heads, HEAD_DIM, rows), jnp.float32),
    ]


def first_row(rows):
    return lax.axis_index("ctx") * rows


def reach_call(offsets, rows):
    def kernel(offsets_ref, far_ref):
        far = jnp.int32(0)
        for i in range(offsets_ref.shape[0] - 1):
            steps = (offsets_ref[i + 1] - 1) // (2 * rows) - offsets_ref[i] // (2 * rows)
            far = jnp.maximum(far, jnp.where(steps >= 2, 1, 0))
        far_ref[0] = far

    return pl.pallas_call(
        kernel,
        out_shape=pltpu.SMEM((1,), jnp.int32),
        in_specs=[smem],
        out_specs=smem,
        name="reach",
    )(in_hbm(offsets))


def own_call(offsets, q, keys, values):
    rows, width = q.shape

    def kernel(offsets_in, q_in, k_in, v_in, starts_ref, q_ref, top_ref, total_ref, acc_ref, offsets_ref, k_ref, v_ref, sems):
        copies = [
            pltpu.make_async_copy(source, target, sems.at[i])
            for i, (source, target) in enumerate(((offsets_in, offsets_ref), (k_in, k_ref), (q_in, q_ref), (v_in, v_ref)))
        ]
        for copy in copies:
            copy.start()
        copies[0].wait()
        first = first_row(rows)
        starts = document_starts(offsets_ref, first, rows)
        starts_ref[...] = starts
        visible = visible_keys(starts, first, rows, first)
        for copy in copies[1:]:
            copy.wait()
        tops, totals, weights, _ = score_block(q_ref, k_ref, visible, None)
        store_rows(top_ref, tops)
        store_rows(total_ref, totals)
        for h, out in enumerate(value_block(v_ref, weights, None, None)):
            acc_ref[h] = out

    outs = pl.pallas_call(
        kernel,
        out_shape=[
            jax.ShapeDtypeStruct((1, rows), jnp.int32),
            jax.ShapeDtypeStruct(q.shape, q.dtype),
            *state_shapes(width // HEAD_DIM, rows),
        ],
        in_specs=[hbm] * 4,
        out_specs=[vmem] * 5,
        scratch_shapes=[
            pltpu.SMEM(offsets.shape, offsets.dtype),
            *[pltpu.VMEM(x.shape, x.dtype) for x in (keys, values)],
            pltpu.SemaphoreType.DMA((4,)),
        ],
        compiler_params=params(),
        cost_estimate=cost(width, rows, 1),
        name="own",
    )(*[in_hbm(x) for x in (offsets, q, keys, values)])
    return *outs[:2], outs[2:]


def cost(width, rows, blocks):
    return pl.CostEstimate(flops=20 * width * rows * rows * blocks, bytes_accessed=0, transcendentals=0)


def reached(back, rows):
    position = lax.axis_index("ctx")
    block = position - back(lax.rem(position, 2))
    return block * rows, (block >= 0) & (block <= position)


def attend_call(starts, q, keys, values, back, state):
    rows, width = q.shape

    def kernel(starts_ref, q_ref, k_ref, v_ref, *refs):
        before, after = refs[:3], refs[3:]
        key_start, seen = reached(back, rows)

        @pl.when(seen)
        def _():
            visible = visible_keys(starts_ref[...], key_start, rows, None)
            tops, totals, weights, alphas = score_block(q_ref, k_ref, visible, before)
            store_rows(after[0], tops)
            store_rows(after[1], totals)
            for h, out in enumerate(value_block(v_ref, weights, alphas, before[2])):
                after[2][h] = out

        @pl.when(jnp.logical_not(seen))
        def _():
            for old, new in zip(before, after):
                new[...] = old[...]

    return pl.pallas_call(
        kernel,
        out_shape=state_shapes(width // HEAD_DIM, rows),
        in_specs=[vmem] * 7,
        out_specs=[vmem] * 3,
        input_output_aliases={4 + i: i for i in range(3)},
        compiler_params=params(),
        cost_estimate=cost(width, rows, 1),
        name="attend",
    )(*in_vmem([starts, q, keys, values, *state]))


def last_scores_call(starts, q, keys, back, state):
    rows, width = q.shape
    heads = width // HEAD_DIM

    def kernel(starts_ref, q_ref, k_ref, top_ref, old_total_ref, total_ref, alpha_ref, weights_ref):
        key_start, seen = reached(back, rows)

        @pl.when(seen)
        def _():
            visible = visible_keys(starts_ref[...], key_start, rows, None)
            _, totals, weights, alphas = score_block(q_ref, k_ref, visible, (top_ref, old_total_ref))
            store_rows(total_ref, totals)
            store_rows(alpha_ref, alphas)
            for h, w in enumerate(weights):
                weights_ref[h] = w

        @pl.when(jnp.logical_not(seen))
        def _():
            total_ref[...] = old_total_ref[...]
            alpha_ref[...] = jnp.ones_like(alpha_ref)
            weights_ref[...] = jnp.zeros_like(weights_ref)

    return pl.pallas_call(
        kernel,
        out_shape=[
            jax.ShapeDtypeStruct((heads, rows), jnp.float32),
            jax.ShapeDtypeStruct((heads, rows), jnp.float32),
            jax.ShapeDtypeStruct((heads, rows, rows), jnp.bfloat16),
        ],
        in_specs=[vmem] * 5,
        out_specs=[vmem] * 3,
        compiler_params=params(),
        cost_estimate=cost(width, rows, 1),
        name="last_scores",
    )(*in_vmem([starts, q, keys, state[0], state[1]]))


def project_into(out_ref, att_ref, w_ref, added_ref, far_core, far_next, part, parts):
    size = out_ref.shape[2]
    block = size * parts
    added_start = 0 if added_ref is None or added_ref.shape[2] == size else part * size
    step = min(size, 256)
    me = lax.axis_index("head")
    bits = (me % 2 + far_core) % 2 + 2 * ((me // 2 + far_next) % 2)
    first = pl.multiple_of(bits * block, block)
    for i in range(out_ref.shape[0]):
        for start in range(0, size, step):
            cut = slice(start, start + step)
            columns = w_ref[:, pl.ds(first + 4 * i * block + part * size + start, step)]
            value = jnp.dot(att_ref[...], columns, preferred_element_type=jnp.float32)
            if added_ref is not None:
                value = value + added_ref[i, :, added_start + start : added_start + start + step].astype(jnp.float32)
            out_ref[i, :, cut] = value.astype(out_ref.dtype)


def by_first_exchange():
    return lax.rem(lax.axis_index("ctx") // 2, 2) == 1


def finish_call(values, weights, totals, alphas, acc, out_weight, count):
    heads, _, rows = acc.shape
    size = out_weight.shape[1] // count // PARTS

    n = len(values)

    def kernel(*refs):
        p_ref, total_ref, alpha_ref, acc_ref, w_ref, att_ref, far_ref = refs[n:]
        v = refs[0][...] if n == 1 else jnp.where(by_first_exchange(), refs[0][...], refs[1][...])
        scales = [alpha_ref[h : h + 1, :] for h in range(heads)]
        outs = value_block(v, [p_ref[h] for h in range(heads)], scales, acc_ref)
        for h, out in enumerate(outs):
            head = out * (1.0 / total_ref[h : h + 1, :])
            att_ref[:, h * HEAD_DIM : (h + 1) * HEAD_DIM] = head.T.astype(jnp.bfloat16)
        project_into(far_ref, att_ref, w_ref, None, 1, 1, 0, PARTS)

    return pl.pallas_call(
        kernel,
        out_shape=[
            jax.ShapeDtypeStruct((rows, heads * HEAD_DIM), jnp.bfloat16),
            jax.ShapeDtypeStruct((count // 4, rows, size), jnp.bfloat16),
        ],
        in_specs=[vmem] * (n + 5),
        out_specs=[vmem] * 2,
        compiler_params=params(),
        name="finish",
    )(*in_vmem([*values, weights, totals, alphas, acc]), out_weight)


def rest_call(attended, out_weight, count):
    rows, depth = attended.shape
    block = out_weight.shape[1] // count

    def kernel(att_ref, w_ref, *refs):
        for part in range(1, PARTS):
            project_into(refs[part - 1], att_ref, w_ref, None, 1, 1, part, PARTS)
        project_into(refs[-1], att_ref, w_ref, None, 1, 0, 0, 1)

    sizes = [block // PARTS] * (PARTS - 1) + [block]
    return pl.pallas_call(
        kernel,
        out_shape=[jax.ShapeDtypeStruct((count // 4, rows, size), jnp.bfloat16) for size in sizes],
        in_specs=[vmem] * 2,
        out_specs=[vmem] * PARTS,
        compiler_params=params(),
        cost_estimate=pl.CostEstimate(flops=2 * rows * depth * sum(sizes) * (count // 4), bytes_accessed=0, transcendentals=0),
        name="rest",
    )(*in_vmem([attended]), out_weight)


def project_call(attended, out_weight, added, far_core, far_next, part, parts, count, out_type, name):
    rows, depth = attended.shape
    size = out_weight.shape[1] // count // parts

    def kernel(att_ref, w_ref, *refs):
        project_into(refs[-1], att_ref, w_ref, refs[0] if len(refs) > 1 else None, far_core, far_next, part, parts)

    more = [] if added is None else [added]
    return pl.pallas_call(
        kernel,
        out_shape=jax.ShapeDtypeStruct((count // 4, rows, size), out_type),
        in_specs=[vmem] * (2 + len(more)),
        out_specs=vmem,
        compiler_params=params(),
        cost_estimate=pl.CostEstimate(flops=2 * rows * depth * size * (count // 4), bytes_accessed=0, transcendentals=0),
        name=name,
    )(*in_vmem([attended]), out_weight, *in_vmem(more))


def output_call(kept, arrived, part, whole):
    rows, size = kept.shape

    def kernel(kept_ref, arrived_ref, *refs):
        out_ref, held, sem = refs[-3:]
        held[...] = (kept_ref[...] + arrived_ref[...].astype(jnp.float32)).T.astype(jnp.bfloat16)
        copy = pltpu.make_async_copy(held, out_ref.at[part * size : (part + 1) * size], sem)
        copy.start()
        copy.wait()

    more = [] if whole is None else [in_hbm(whole)]
    return pl.pallas_call(
        kernel,
        out_shape=jax.ShapeDtypeStruct((size * PARTS, rows), jnp.bfloat16),
        in_specs=[vmem] * 2 + [hbm] * len(more),
        out_specs=hbm,
        scratch_shapes=[pltpu.VMEM((size, rows), jnp.bfloat16), pltpu.SemaphoreType.DMA],
        input_output_aliases={2: 0} if more else {},
        compiler_params=params(),
        name="output",
    )(*in_vmem([kept, arrived]), *more)


def swapped(array, axis, bit):
    return lax.ppermute(array, axis, [(i, i ^ bit) for i in range(lax.axis_size(axis))])


def summed_over_heads(attended, far, out_weight, count):
    def project(added, far_core, far_next, part, parts, out_type, name):
        return project_call(attended, out_weight, added, far_core, far_next, part, parts, count, out_type, name)

    *fars, near = rest_call(attended, out_weight, count)
    got_fars = [swapped(x, "head", 1) for x in (far, *fars)]
    sents = [project(got_fars[part], 0, 1, part, PARTS, jnp.bfloat16, "sent") for part in range(PARTS)]
    gots = [swapped(x, "head", 2) for x in sents]
    got_near = swapped(near, "head", 1)
    kepts = [project(got_near, 0, 0, part, PARTS, jnp.float32, "kept") for part in range(PARTS)]
    me = lax.axis_index("head")
    whole = None
    for part, (kept, got) in enumerate(zip(kepts, gots)):
        for b in range(2, count.bit_length() - 1):
            kept = kept + got.astype(jnp.float32)
            pairs = kept.reshape(kept.shape[0] // 2, 2, *kept.shape[1:])
            bit = (me >> b) & 1
            sent = lax.dynamic_index_in_dim(pairs, 1 - bit, 1, keepdims=False)
            kept = lax.dynamic_index_in_dim(pairs, bit, 1, keepdims=False)
            got = swapped(sent.astype(jnp.bfloat16), "head", 1 << b)
        whole = output_call(kept[0], got[0], part, whole)
    return whole


def on_device(queries, key_vectors, value_vectors, out_weight, offsets):
    devices = lax.axis_size("ctx")
    heads = lax.axis_size("head")
    rows = queries.shape[0]
    pair_steps = (min(REACH, devices // 2) + 1) // 2

    def moved_by(array, target):
        route = []
        for position in range(devices):
            for head in range(heads):
                p, x, h = target(position // 2, position % 2, head)
                route.append((position * heads + head, (2 * p + x) * heads + h))
        return lax.ppermute(array, ("ctx", "head"), route)

    def shifted(pair, step):
        last = devices // 2 - 1

        def target(p, x, h):
            return (p, x, h ^ 1) if p < step - 1 else (p + 1 if p < last else step - 1, x, h)

        return tuple(moved_by(m, target) for m in pair)

    def across(pair, step):
        return tuple(moved_by(m, lambda p, x, h: (p, x, h ^ 1) if p < step else (p, 1 - x, h)) for m in pair)

    def exchanged(array):
        pairs = devices // 2

        def target(shift, p, x, h):
            other = ((p + shift) ^ 1) - shift
            return (other, x, h) if 0 <= other < pairs else (p, x, h ^ 1)

        return tuple(moved_by(array, lambda p, x, h, shift=shift: target(shift, p, x, h)) for shift in (0, 1))

    def after(pair, state):
        first, state = lax.optimization_barrier((pair[0], state))
        return (first, pair[1]), state

    def finished(starts, q, pair, back, state, out_weight):
        totals, alphas, weights = last_scores_call(starts, q, pair[0], back, state)
        attended, product = finish_call(pair[1:], weights, totals, alphas, state[2], out_weight, heads)
        return summed_over_heads(attended, product, out_weight, heads)

    def near(queries, key_vectors, value_vectors, out_weight, offsets):
        own = (key_vectors, value_vectors)
        moved = shifted(own, 1)
        beside = across(own, 0)
        starts, q, state = own_call(offsets, queries, key_vectors, value_vectors)
        moved, state = after(moved, state)
        crossed = across(moved[:1], 1) + exchanged(beside[1])
        state = attend_call(starts, q, *moved, lambda x: 2, state)
        state = attend_call(starts, q, *beside, lambda x: 2 * x - 1, state)
        return finished(starts, q, crossed, lambda x: 1 + 2 * x, state, out_weight)

    def reaching(queries, key_vectors, value_vectors, out_weight, offsets):
        moved = (key_vectors, value_vectors)
        beside = across(moved, 0)
        starts, q, state = own_call(offsets, queries, key_vectors, value_vectors)
        waiting = [(*beside, lambda x: 2 * x - 1)]
        for step in range(1, pair_steps + 1):
            moved, state = after(shifted(moved, step), state)
            waiting.insert(0, (*moved, lambda x, step=step: 2 * step))
            crossed = across(moved, step)
            if step < pair_steps:
                for piece in waiting:
                    state = attend_call(starts, q, *piece, state)
                waiting = [(*crossed, lambda x, step=step: 2 * step - 1 + 2 * x)]
        for piece in waiting:
            state = attend_call(starts, q, *piece, state)
        return finished(starts, q, crossed, lambda x: 2 * pair_steps - 1 + 2 * x, state, out_weight)

    given = (queries, key_vectors, value_vectors, out_weight, offsets)
    if pair_steps == 1:
        return near(*given)
    return lax.cond(reach_call(offsets, rows)[0] > 0, reaching, near, *given)


def solution(mesh):
    placed = (P("ctx", "head"), P("ctx", "head"), P("ctx", "head"), P("head", None), P())
    return jax.shard_map(
        on_device, mesh=mesh, in_specs=placed, out_specs=P("head", "ctx"), check_vma=False
    )
```

profile of v0, /device:TPU:0, one launch (start us, length us, event | category | flops | bytes accessed | tf_op | source)
XLA Modules:
  0.0 34.5 jit_solution(17479478758861774103)
XLA Ops:
  0.0 0.7 %reach.1 = s32[1]{0:T(128)S(4)} custom-call(s32[5]{0:T(128)} %offsets_ref.1), custom_call_target="tpu_custom_call" | custom-call | tf_op jit(solution)/shard_map/reach/pallas_call | solution.py:111
  0.7 33.6 %conditional.1 = (bf16[1024,256]{1,0:T(8,128)(2,1)}) conditional(s32[]{:T(128)} %bitcast.8, (bf16[256,256]{1,0:T(8,128)(2,1)}, s32[5]{0:T(128)}, bf16[256,1024]{1,0:T(8,128)(2,1)}, bf16[256,256]{1,0:T(8,128)(2,1)}, bf16[1024,4096]{1,0:T(8,128)(2,1)}) %tuple.14, (bf16[256,256]{1,0:T(8,128)(2,1)}, s32[5]{0:T(128)}, bf16[256,1024]{1,0:T(8,128)(2,1)}, ...), branch_computations={%region_0.0_spmd, %region_1.0_spmd} | conditional | flops 9932111872 | bytes 36700816 | solution.py:460
  0.7 3.1 %collective-permute-start.3 = (bf16[256,256]{1,0:T(8,128)(2,1)}, bf16[256,256]{1,0:T(8,128)(2,1)S(1)}, u32[]{:S(2)}, u32[]{:S(2)}) collective-permute-start(bf16[256,256]{1,0:T(8,128)(2,1)} %get-tuple-element.105.k_in), channel_id=1, source_target_pairs={{0,8},{1,9},{2,10},{3,11},{4,12},{5,13},{6,14},{7,15},{8,16},{9,17... | collective-permute-start | bytes 393224 | tf_op jit(solution)/shard_map/cond/branch_0_fun/ppermute | solution.py:398
  3.8 1.5 %collective-permute-start = (bf16[256,256]{1,0:T(8,128)(2,1)}, bf16[256,256]{1,0:T(8,128)(2,1)S(1)}, u32[]{:S(2)}, u32[]{:S(2)}) collective-permute-start(bf16[256,256]{1,0:T(8,128)(2,1)} %get-tuple-element.101.v_in), channel_id=1, source_target_pairs={{0,4},{1,5},{2,6},{3,7},{4,0},{5,1},{6,2},{7,3},{8,12},{9,13},{10,... | collective-permute-start | bytes 393224 | tf_op jit(solution)/shard_map/cond/branch_0_fun/ppermute | solution.py:398
  5.3 1.6 %collective-permute-start.6 = (bf16[256,256]{1,0:T(8,128)(2,1)}, bf16[256,256]{1,0:T(8,128)(2,1)S(1)}, u32[]{:S(2)}, u32[]{:S(2)}) collective-permute-start(bf16[256,256]{1,0:T(8,128)(2,1)} %get-tuple-element.101.v_in), channel_id=1, source_target_pairs={{0,8},{1,9},{2,10},{3,11},{4,12},{5,13},{6,14},{7,15},{8,16},{9,17... | collective-permute-start | bytes 393224 | tf_op jit(solution)/shard_map/cond/branch_0_fun/ppermute | solution.py:398
  6.9 0.5 %collective-permute-start.5 = (bf16[256,256]{1,0:T(8,128)(2,1)}, bf16[256,256]{1,0:T(8,128)(2,1)S(1)}, u32[]{:S(2)}, u32[]{:S(2)}) collective-permute-start(bf16[256,256]{1,0:T(8,128)(2,1)} %get-tuple-element.105.k_in), channel_id=1, source_target_pairs={{0,4},{1,5},{2,6},{3,7},{4,0},{5,1},{6,2},{7,3},{8,12},{9,13},{10,... | collective-permute-start | bytes 393224 | tf_op jit(solution)/shard_map/cond/branch_0_fun/ppermute | solution.py:398
  7.4 0.0 slice-start
  7.4 2.4 %own.2 = (s32[1,256]{1,0:T(1,128)S(1)}, bf16[256,1024]{1,0:T(8,128)(2,1)S(1)}, f32[8,256]{1,0:T(8,128)S(1)}, f32[8,256]{1,0:T(8,128)S(1)}, f32[8,128,256]{2,1,0:T(8,128)S(1)}) custom-call(s32[5]{0:T(128)} %get-tuple-element.29.offsets_in, bf16[256,1024]{1,0:T(8,128)(2,1)} %get-tuple-element.103.q_in, bf16[256,256]{1,0:T(8,128)(2,1)} %get-tuple-element.105.k_in, ...), custom_call_target="tpu_custom_call" | custom-call | flops 1342177280 | tf_op jit(solution)/shard_map/cond/branch_0_fun/own/pallas_call | solution.py:143
  9.8 0.0 collective-permute-done.3.k_ref
  9.8 0.0 collective-permute-start.4
  9.9 0.0 collective-permute-done.v_ref
  9.9 3.0 %collective-permute-start.1 = (bf16[256,256]{1,0:T(8,128)(2,1)S(1)}, bf16[256,256]{1,0:T(8,128)(2,1)S(1)}, u32[]{:S(2)}, u32[]{:S(2)}) collective-permute-start(bf16[256,256]{1,0:T(8,128)(2,1)S(1)} %collective-permute-done.v_ref), channel_id=1, source_target_pairs={{0,8},{1,9},{2,10},{3,11},{4,12},{5,13},{6,14},{7,15},{8,0},{9,1},... | collective-permute-start | bytes 393224 | tf_op jit(solution)/shard_map/cond/branch_0_fun/ppermute | solution.py:398
  12.9 0.0 collective-permute-start.2
  12.9 0.0 collective-permute-done.6.v_ref
  12.9 0.1 attend.6
  13.1 0.0 collective-permute-done.5.k_ref
  13.1 0.0 slice-start.1
  13.1 0.2 attend.7
  13.3 0.0 collective-permute-done.4.k_ref
  13.3 0.1 last_scores.2
  13.4 2.5 %collective-permute-done.1.refs_0_ = bf16[256,256]{1,0:T(8,128)(2,1)S(1)} collective-permute-done((bf16[256,256]{1,0:T(8,128)(2,1)S(1)}, bf16[256,256]{1,0:T(8,128)(2,1)S(1)}, u32[]{:S(2)}, u32[]{:S(2)}) %collective-permute-start.1) | collective-permute-done | bytes 131104 | tf_op jit(solution)/shard_map/cond/branch_0_fun/ppermute | solution.py:398
  15.9 0.0 collective-permute-done.2.refs_1_
  15.9 0.0 slice-done
  15.9 0.0 slice-done.1
  15.9 0.8 %finish.2 = (bf16[256,1024]{1,0:T(8,128)(2,1)S(1)}, bf16[1,256,512]{2,1,0:T(8,128)(2,1)S(1)}) custom-call(bf16[256,256]{1,0:T(8,128)(2,1)S(1)} %collective-permute-done.1.refs_0_, bf16[256,256]{1,0:T(8,128)(2,1)S(1)} %collective-permute-done.2.refs_1_, bf16[8,256,256]{2,1,0:T(8,128)(2,1)S(1)} %get-tuple-element.46.refs_2_, ...), custom_call_target="tpu_custom_call" | custom-call | tf_op jit(solution)/shard_map/cond/branch_0_fun/finish/pallas_call | solution.py:282
  16.7 0.1 collective-permute-start.10
  16.8 1.0 %rest.2 = (bf16[1,256,512]{2,1,0:T(8,128)(2,1)S(1)}, bf16[1,256,1024]{2,1,0:T(8,128)(2,1)S(1)}) custom-call(bf16[256,1024]{1,0:T(8,128)(2,1)S(1)} %get-tuple-element.51.att_ref, bf16[1024,4096]{1,0:T(8,128)(2,1)S(1)} %bitcast.18), custom_call_target="tpu_custom_call" | custom-call | flops 805306368 | tf_op jit(solution)/shard_map/cond/branch_0_fun/rest/pallas_call | solution.py:305
  17.8 0.5 %collective-permute-start.7 = (bf16[1,256,1024]{2,1,0:T(8,128)(2,1)S(1)}, bf16[1,256,1024]{2,1,0:T(8,128)(2,1)S(1)}, u32[]{:S(2)}, u32[]{:S(2)}) collective-permute-start(bf16[1,256,1024]{2,1,0:T(8,128)(2,1)S(1)} %get-tuple-element.52), channel_id=1, source_target_pairs={{0,1},{1,0},{2,3},{3,2},{4,5},{5,4},{6,7},{7,6},{8,9},{9,8},{10,11... | collective-permute-start | bytes 1572872 | tf_op jit(solution)/shard_map/cond/branch_0_fun/ppermute | solution.py:359
  18.4 0.1 collective-permute-start.8
  18.4 0.0 collective-permute-done.10.refs_0_
  18.4 0.5 %sent.5 = bf16[1,256,512]{2,1,0:T(8,128)(2,1)S(1)} custom-call(bf16[256,1024]{1,0:T(8,128)(2,1)S(1)} %get-tuple-element.51.att_ref, bf16[1024,4096]{1,0:T(8,128)(2,1)S(1)} %bitcast.18, bf16[1,256,512]{2,1,0:T(8,128)(2,1)S(1)} %collective-permute-done.10.refs_0_), custom_call_target="tpu_custom_call" | custom-call | flops 268435456 | tf_op jit(solution)/shard_map/cond/branch_0_fun/sent/pallas_call | solution.py:324
  18.9 1.6 %collective-permute-start.11 = (bf16[1,256,512]{2,1,0:T(8,128)(2,1)S(1)}, bf16[1,256,512]{2,1,0:T(8,128)(2,1)S(1)}, u32[]{:S(2)}, u32[]{:S(2)}) collective-permute-start(bf16[1,256,512]{2,1,0:T(8,128)(2,1)S(1)} %sent.5), channel_id=1, source_target_pairs={{0,2},{1,3},{2,0},{3,1},{4,6},{5,7},{6,4},{7,5},{8,10},{9,11},{10,... | collective-permute-start | bytes 786440 | tf_op jit(solution)/shard_map/cond/branch_0_fun/ppermute | solution.py:359
  20.5 0.0 collective-permute-done.8.refs_0_
  20.5 0.5 %sent.4 = bf16[1,256,512]{2,1,0:T(8,128)(2,1)S(1)} custom-call(bf16[256,1024]{1,0:T(8,128)(2,1)S(1)} %get-tuple-element.51.att_ref, bf16[1024,4096]{1,0:T(8,128)(2,1)S(1)} %bitcast.18, bf16[1,256,512]{2,1,0:T(8,128)(2,1)S(1)} %collective-permute-done.8.refs_0_), custom_call_target="tpu_custom_call" | custom-call | flops 268435456 | tf_op jit(solution)/shard_map/cond/branch_0_fun/sent/pallas_call | solution.py:324
  21.0 1.4 %collective-permute-start.9 = (bf16[1,256,512]{2,1,0:T(8,128)(2,1)S(1)}, bf16[1,256,512]{2,1,0:T(8,128)(2,1)S(1)}, u32[]{:S(2)}, u32[]{:S(2)}) collective-permute-start(bf16[1,256,512]{2,1,0:T(8,128)(2,1)S(1)} %sent.4), channel_id=1, source_target_pairs={{0,2},{1,3},{2,0},{3,1},{4,6},{5,7},{6,4},{7,5},{8,10},{9,11},{10,... | collective-permute-start | bytes 786440 | tf_op jit(solution)/shard_map/cond/branch_0_fun/ppermute | solution.py:359
  22.4 0.0 collective-permute-done.7.refs_0_
  22.4 0.5 %kept.5 = f32[1,256,512]{2,1,0:T(8,128)S(1)} custom-call(bf16[256,1024]{1,0:T(8,128)(2,1)S(1)} %get-tuple-element.51.att_ref, bf16[1024,4096]{1,0:T(8,128)(2,1)S(1)} %bitcast.18, bf16[1,256,1024]{2,1,0:T(8,128)(2,1)S(1)} %collective-permute-done.7.refs_0_), custom_call_target="tpu_custom_call" | custom-call | flops 268435456 | tf_op jit(solution)/shard_map/cond/branch_0_fun/kept/pallas_call | solution.py:324
  22.8 5.3 %collective-permute-done.11 = bf16[1,256,512]{2,1,0:T(8,128)(2,1)S(1)} collective-permute-done((bf16[1,256,512]{2,1,0:T(8,128)(2,1)S(1)}, bf16[1,256,512]{2,1,0:T(8,128)(2,1)S(1)}, u32[]{:S(2)}, u32[]{:S(2)}) %collective-permute-start.11) | collective-permute-done | bytes 262176 | tf_op jit(solution)/shard_map/cond/branch_0_fun/ppermute | solution.py:359
  28.1 0.8 %output.4.refs_0_ = bf16[1024,256]{1,0:T(8,128)(2,1)} custom-call(f32[256,512]{1,0:T(8,128)S(1)} %bitcast.11, bf16[256,512]{1,0:T(8,128)(2,1)S(1)} %bitcast.13), custom_call_target="tpu_custom_call" | custom-call | tf_op jit(solution)/shard_map/cond/branch_0_fun/output/pallas_call | solution.py:346
  29.0 0.5 %kept.4 = f32[1,256,512]{2,1,0:T(8,128)S(1)} custom-call(bf16[256,1024]{1,0:T(8,128)(2,1)S(1)} %get-tuple-element.51.att_ref, bf16[1024,4096]{1,0:T(8,128)(2,1)S(1)} %bitcast.18, bf16[1,256,1024]{2,1,0:T(8,128)(2,1)S(1)} %collective-permute-done.7.refs_0_), custom_call_target="tpu_custom_call" | custom-call | flops 268435456 | tf_op jit(solution)/shard_map/cond/branch_0_fun/kept/pallas_call | solution.py:324
  29.5 3.8 %collective-permute-done.9 = bf16[1,256,512]{2,1,0:T(8,128)(2,1)S(1)} collective-permute-done((bf16[1,256,512]{2,1,0:T(8,128)(2,1)S(1)}, bf16[1,256,512]{2,1,0:T(8,128)(2,1)S(1)}, u32[]{:S(2)}, u32[]{:S(2)}) %collective-permute-start.9) | collective-permute-done | bytes 262176 | tf_op jit(solution)/shard_map/cond/branch_0_fun/ppermute | solution.py:359
  33.3 0.8 %output.5 = bf16[1024,256]{1,0:T(8,128)(2,1)} custom-call(f32[256,512]{1,0:T(8,128)S(1)} %bitcast.9, bf16[256,512]{1,0:T(8,128)(2,1)S(1)} %bitcast.14, bf16[1024,256]{1,0:T(8,128)(2,1)} %output.4.refs_0_), custom_call_target="tpu_custom_call", output_to_operand_aliasing={{}: (2, {})} | custom-call | tf_op jit(solution)/shard_map/cond/branch_0_fun/output/pallas_call | solution.py:346
  (1 shorter events, 0.0 us)
Async XLA Ops:
  0.7 9.1 %collective-permute-start.3 = (bf16[256,256]{1,0:T(8,128)(2,1)}, bf16[256,256]{1,0:T(8,128)(2,1)S(1)}, u32[]{:S(2)}, u32[]{:S(2)}) collective-permute-start(bf16[256,256]{1,0:T(8,128)(2,1)} %get-tuple-element.105.k_in), channel_id=1, source_target_pairs={{0,8},{1,9},{2,10},{3,11},{4,12},{5,13},{6,14},{7,15},{8,16},{9,17... | collective-permute-start | bytes 393224 | tf_op jit(solution)/shard_map/cond/branch_0_fun/ppermute | solution.py:398
  3.8 6.1 %collective-permute-start = (bf16[256,256]{1,0:T(8,128)(2,1)}, bf16[256,256]{1,0:T(8,128)(2,1)S(1)}, u32[]{:S(2)}, u32[]{:S(2)}) collective-permute-start(bf16[256,256]{1,0:T(8,128)(2,1)} %get-tuple-element.101.v_in), channel_id=1, source_target_pairs={{0,4},{1,5},{2,6},{3,7},{4,0},{5,1},{6,2},{7,3},{8,12},{9,13},{10,... | collective-permute-start | bytes 393224 | tf_op jit(solution)/shard_map/cond/branch_0_fun/ppermute | solution.py:398
  5.3 7.6 %collective-permute-start.6 = (bf16[256,256]{1,0:T(8,128)(2,1)}, bf16[256,256]{1,0:T(8,128)(2,1)S(1)}, u32[]{:S(2)}, u32[]{:S(2)}) collective-permute-start(bf16[256,256]{1,0:T(8,128)(2,1)} %get-tuple-element.101.v_in), channel_id=1, source_target_pairs={{0,8},{1,9},{2,10},{3,11},{4,12},{5,13},{6,14},{7,15},{8,16},{9,17... | collective-permute-start | bytes 393224 | tf_op jit(solution)/shard_map/cond/branch_0_fun/ppermute | solution.py:398
  6.9 6.2 %collective-permute-start.5 = (bf16[256,256]{1,0:T(8,128)(2,1)}, bf16[256,256]{1,0:T(8,128)(2,1)S(1)}, u32[]{:S(2)}, u32[]{:S(2)}) collective-permute-start(bf16[256,256]{1,0:T(8,128)(2,1)} %get-tuple-element.105.k_in), channel_id=1, source_target_pairs={{0,4},{1,5},{2,6},{3,7},{4,0},{5,1},{6,2},{7,3},{8,12},{9,13},{10,... | collective-permute-start | bytes 393224 | tf_op jit(solution)/shard_map/cond/branch_0_fun/ppermute | solution.py:398
  7.4 8.5 %slice-start = ((s8[8388608]{0:T(1024)(128)(4,1)}), s8[4194304]{0:T(1024)(128)(4,1)S(1)}, s32[]{:S(2)}) async-start(s8[8388608]{0:T(1024)(128)(4,1)} %bitcast.17), calls=%async_computation | async-start | bytes 8388608 | tf_op jit(solution)/shard_map/cond
  9.8 3.4 %collective-permute-start.4 = (bf16[256,256]{1,0:T(8,128)(2,1)S(1)}, bf16[256,256]{1,0:T(8,128)(2,1)S(1)}, u32[]{:S(2)}, u32[]{:S(2)}) collective-permute-start(bf16[256,256]{1,0:T(8,128)(2,1)S(1)} %collective-permute-done.3.k_ref), channel_id=1, source_target_pairs={{0,1},{1,0},{2,3},{3,2},{4,5},{5,4},{6,7},{7,6},{8,12},{9,13},{10,... | collective-permute-start | bytes 393224 | tf_op jit(solution)/shard_map/cond/branch_0_fun/ppermute | solution.py:398
  9.9 6.0 %collective-permute-start.1 = (bf16[256,256]{1,0:T(8,128)(2,1)S(1)}, bf16[256,256]{1,0:T(8,128)(2,1)S(1)}, u32[]{:S(2)}, u32[]{:S(2)}) collective-permute-start(bf16[256,256]{1,0:T(8,128)(2,1)S(1)} %collective-permute-done.v_ref), channel_id=1, source_target_pairs={{0,8},{1,9},{2,10},{3,11},{4,12},{5,13},{6,14},{7,15},{8,0},{9,1},... | collective-permute-start | bytes 393224 | tf_op jit(solution)/shard_map/cond/branch_0_fun/ppermute | solution.py:398
  12.9 2.9 %collective-permute-start.2 = (bf16[256,256]{1,0:T(8,128)(2,1)S(1)}, bf16[256,256]{1,0:T(8,128)(2,1)S(1)}, u32[]{:S(2)}, u32[]{:S(2)}) collective-permute-start(bf16[256,256]{1,0:T(8,128)(2,1)S(1)} %collective-permute-done.v_ref), channel_id=1, source_target_pairs={{0,1},{1,0},{2,3},{3,2},{4,5},{5,4},{6,7},{7,6},{8,16},{9,17},{10,... | collective-permute-start | bytes 393224 | tf_op jit(solution)/shard_map/cond/branch_0_fun/ppermute | solution.py:398
  13.1 2.8 %slice-start.1 = ((s8[8388608]{0:T(1024)(128)(4,1)}), s8[4194304]{0:T(1024)(128)(4,1)S(1)}, s32[]{:S(2)}) async-start(s8[8388608]{0:T(1024)(128)(4,1)} %bitcast.17), calls=%async_computation.1 | async-start | bytes 8388608 | tf_op jit(solution)/shard_map/cond
  16.7 1.8 %collective-permute-start.10 = (bf16[1,256,512]{2,1,0:T(8,128)(2,1)S(1)}, bf16[1,256,512]{2,1,0:T(8,128)(2,1)S(1)}, u32[]{:S(2)}, u32[]{:S(2)}) collective-permute-start(bf16[1,256,512]{2,1,0:T(8,128)(2,1)S(1)} %get-tuple-element.54), channel_id=1, source_target_pairs={{0,1},{1,0},{2,3},{3,2},{4,5},{5,4},{6,7},{7,6},{8,9},{9,8},{10,11... | collective-permute-start | bytes 786440 | tf_op jit(solution)/shard_map/cond/branch_0_fun/ppermute | solution.py:359
  17.8 4.5 %collective-permute-start.7 = (bf16[1,256,1024]{2,1,0:T(8,128)(2,1)S(1)}, bf16[1,256,1024]{2,1,0:T(8,128)(2,1)S(1)}, u32[]{:S(2)}, u32[]{:S(2)}) collective-permute-start(bf16[1,256,1024]{2,1,0:T(8,128)(2,1)S(1)} %get-tuple-element.52), channel_id=1, source_target_pairs={{0,1},{1,0},{2,3},{3,2},{4,5},{5,4},{6,7},{7,6},{8,9},{9,8},{10,11... | collective-permute-start | bytes 1572872 | tf_op jit(solution)/shard_map/cond/branch_0_fun/ppermute | solution.py:359
  18.4 2.1 %collective-permute-start.8 = (bf16[1,256,512]{2,1,0:T(8,128)(2,1)S(1)}, bf16[1,256,512]{2,1,0:T(8,128)(2,1)S(1)}, u32[]{:S(2)}, u32[]{:S(2)}) collective-permute-start(bf16[1,256,512]{2,1,0:T(8,128)(2,1)S(1)} %get-tuple-element.53), channel_id=1, source_target_pairs={{0,1},{1,0},{2,3},{3,2},{4,5},{5,4},{6,7},{7,6},{8,9},{9,8},{10,11... | collective-permute-start | bytes 786440 | tf_op jit(solution)/shard_map/cond/branch_0_fun/ppermute | solution.py:359
  18.9 9.2 %collective-permute-start.11 = (bf16[1,256,512]{2,1,0:T(8,128)(2,1)S(1)}, bf16[1,256,512]{2,1,0:T(8,128)(2,1)S(1)}, u32[]{:S(2)}, u32[]{:S(2)}) collective-permute-start(bf16[1,256,512]{2,1,0:T(8,128)(2,1)S(1)} %sent.5), channel_id=1, source_target_pairs={{0,2},{1,3},{2,0},{3,1},{4,6},{5,7},{6,4},{7,5},{8,10},{9,11},{10,... | collective-permute-start | bytes 786440 | tf_op jit(solution)/shard_map/cond/branch_0_fun/ppermute | solution.py:359
  21.0 12.3 %collective-permute-start.9 = (bf16[1,256,512]{2,1,0:T(8,128)(2,1)S(1)}, bf16[1,256,512]{2,1,0:T(8,128)(2,1)S(1)}, u32[]{:S(2)}, u32[]{:S(2)}) collective-permute-start(bf16[1,256,512]{2,1,0:T(8,128)(2,1)S(1)} %sent.4), channel_id=1, source_target_pairs={{0,2},{1,3},{2,0},{3,1},{4,6},{5,7},{6,4},{7,5},{8,10},{9,11},{10,... | collective-permute-start | bytes 786440 | tf_op jit(solution)/shard_map/cond/branch_0_fun/ppermute | solution.py:359
where the time goes:
time: 34.7 us; the launch traced here: 34.5 us
  starting transfers between devices  13.4 us (39%)
  waiting for transfers between devices  11.6 us (33%)
  Pallas kernels  8.9 us (26%)
  loops' own time  0.39 us (1%)
    ppermute x7, starting transfers between devices, moved_by(): return lax.ppermute(array, ('ctx', 'head'), route)  9.76 us
    ppermute x5, waiting for transfers between devices, swapped(): lax.ppermute(array, axis, [(i, i ^ bit) for i in range(lax.axis_size(axis...  9.08 us
    ppermute x5, starting transfers between devices, swapped(): lax.ppermute(array, axis, [(i, i ^ bit) for i in range(lax.axis_size(axis...  3.64 us
    ppermute x7, waiting for transfers between devices, moved_by(): return lax.ppermute(array, ('ctx', 'head'), route)  2.55 us
    pallas_call x1, Pallas kernels, own_call(): pl.pallas_call(kernel, out_shape=[jax.ShapeDtypeStruct((1, rows), jnp.int...  2.37 us
    pallas_call x4, Pallas kernels, project_call(): pl.pallas_call(kernel, out_shape=jax.ShapeDtypeStruct((count // 4, rows,...  1.9 us
    pallas_call x2, Pallas kernels, output_call(): pl.pallas_call(kernel, out_shape=jax.ShapeDtypeStruct((size * PARTS, rows...  1.7 us
    pallas_call x1, Pallas kernels, rest_call(): pl.pallas_call(kernel, out_shape=[jax.ShapeDtypeStruct((count // 4, rows,...  1.04 us
  transfers between devices with their start and end apart: 12, of which 3 were waited for; matrix products, arithmetic and copies ran while one was open for 0% of the time, Pallas kernels for 19%

commit v1 on v0

--- a/solution.py
+++ b/solution.py
@@ -444,7 +444,7 @@
         waiting = [(*beside, lambda x: 2 * x - 1)]
         for step in range(1, pair_steps + 1):
             moved, state = after(shifted(moved, step), state)
-            waiting.insert(0, (*moved, lambda x, step=step: 2 * step))
+            waiting.insert(0 if step == 1 else 1, (*moved, lambda x, step=step: 2 * step))
             crossed = across(moved, step)
             if step < pair_steps:
                 for piece in waiting:

time: 34.7 us -> 34.7 us (level)
  no operation moved by 1% of the time
where the time goes in v1:
time: 34.7 us; the launch traced here: 34.5 us
  starting transfers between devices  13.4 us (39%)
  waiting for transfers between devices  11.6 us (33%)
  Pallas kernels  8.9 us (26%)
  loops' own time  0.39 us (1%)
    ppermute x7, starting transfers between devices, moved_by(): return lax.ppermute(array, ('ctx', 'head'), route)  9.76 us
    ppermute x5, waiting for transfers between devices, swapped(): lax.ppermute(array, axis, [(i, i ^ bit) for i in range(lax.axis_size(axis...  9.08 us
    ppermute x5, starting transfers between devices, swapped(): lax.ppermute(array, axis, [(i, i ^ bit) for i in range(lax.axis_size(axis...  3.64 us
    ppermute x7, waiting for transfers between devices, moved_by(): return lax.ppermute(array, ('ctx', 'head'), route)  2.55 us
    pallas_call x1, Pallas kernels, own_call(): pl.pallas_call(kernel, out_shape=[jax.ShapeDtypeStruct((1, rows), jnp.int...  2.37 us
    pallas_call x4, Pallas kernels, project_call(): pl.pallas_call(kernel, out_shape=jax.ShapeDtypeStruct((count // 4, rows,...  1.9 us
    pallas_call x2, Pallas kernels, output_call(): pl.pallas_call(kernel, out_shape=jax.ShapeDtypeStruct((size * PARTS, rows...  1.7 us
    pallas_call x1, Pallas kernels, rest_call(): pl.pallas_call(kernel, out_shape=[jax.ShapeDtypeStruct((count // 4, rows,...  1.04 us
  transfers between devices with their start and end apart: 12, of which 3 were waited for; matrix products, arithmetic and copies ran while one was open for 0% of the time, Pallas kernels for 19%

profile of v1, /device:TPU:0, one launch (start us, length us, event | category | flops | bytes accessed | tf_op | source)
XLA Modules:
  0.0 34.5 jit_solution(982635355236171192)
XLA Ops:
  0.0 0.7 %reach.1 = s32[1]{0:T(128)S(4)} custom-call(s32[5]{0:T(128)} %offsets_ref.1), custom_call_target="tpu_custom_call" | custom-call | tf_op jit(solution)/shard_map/reach/pallas_call | solution.py:111
  0.7 33.6 %conditional.1 = (bf16[1024,256]{1,0:T(8,128)(2,1)}) conditional(s32[]{:T(128)} %bitcast.8, (bf16[256,256]{1,0:T(8,128)(2,1)}, s32[5]{0:T(128)}, bf16[256,1024]{1,0:T(8,128)(2,1)}, bf16[256,256]{1,0:T(8,128)(2,1)}, bf16[1024,4096]{1,0:T(8,128)(2,1)}) %tuple.14, (bf16[256,256]{1,0:T(8,128)(2,1)}, s32[5]{0:T(128)}, bf16[256,1024]{1,0:T(8,128)(2,1)}, ...), branch_computations={%region_0.0_spmd, %region_1.0_spmd} | conditional | flops 9932111872 | bytes 36700816 | solution.py:460
  0.7 3.1 %collective-permute-start.3 = (bf16[256,256]{1,0:T(8,128)(2,1)}, bf16[256,256]{1,0:T(8,128)(2,1)S(1)}, u32[]{:S(2)}, u32[]{:S(2)}) collective-permute-start(bf16[256,256]{1,0:T(8,128)(2,1)} %get-tuple-element.105.k_in), channel_id=1, source_target_pairs={{0,8},{1,9},{2,10},{3,11},{4,12},{5,13},{6,14},{7,15},{8,16},{9,17... | collective-permute-start | bytes 393224 | tf_op jit(solution)/shard_map/cond/branch_0_fun/ppermute | solution.py:398
  3.8 1.5 %collective-permute-start = (bf16[256,256]{1,0:T(8,128)(2,1)}, bf16[256,256]{1,0:T(8,128)(2,1)S(1)}, u32[]{:S(2)}, u32[]{:S(2)}) collective-permute-start(bf16[256,256]{1,0:T(8,128)(2,1)} %get-tuple-element.101.v_in), channel_id=1, source_target_pairs={{0,4},{1,5},{2,6},{3,7},{4,0},{5,1},{6,2},{7,3},{8,12},{9,13},{10,... | collective-permute-start | bytes 393224 | tf_op jit(solution)/shard_map/cond/branch_0_fun/ppermute | solution.py:398
  5.3 1.6 %collective-permute-start.6 = (bf16[256,256]{1,0:T(8,128)(2,1)}, bf16[256,256]{1,0:T(8,128)(2,1)S(1)}, u32[]{:S(2)}, u32[]{:S(2)}) collective-permute-start(bf16[256,256]{1,0:T(8,128)(2,1)} %get-tuple-element.101.v_in), channel_id=1, source_target_pairs={{0,8},{1,9},{2,10},{3,11},{4,12},{5,13},{6,14},{7,15},{8,16},{9,17... | collective-permute-start | bytes 393224 | tf_op jit(solution)/shard_map/cond/branch_0_fun/ppermute | solution.py:398
  6.9 0.5 %collective-permute-start.5 = (bf16[256,256]{1,0:T(8,128)(2,1)}, bf16[256,256]{1,0:T(8,128)(2,1)S(1)}, u32[]{:S(2)}, u32[]{:S(2)}) collective-permute-start(bf16[256,256]{1,0:T(8,128)(2,1)} %get-tuple-element.105.k_in), channel_id=1, source_target_pairs={{0,4},{1,5},{2,6},{3,7},{4,0},{5,1},{6,2},{7,3},{8,12},{9,13},{10,... | collective-permute-start | bytes 393224 | tf_op jit(solution)/shard_map/cond/branch_0_fun/ppermute | solution.py:398
  7.4 0.0 slice-start
  7.4 2.4 %own.2 = (s32[1,256]{1,0:T(1,128)S(1)}, bf16[256,1024]{1,0:T(8,128)(2,1)S(1)}, f32[8,256]{1,0:T(8,128)S(1)}, f32[8,256]{1,0:T(8,128)S(1)}, f32[8,128,256]{2,1,0:T(8,128)S(1)}) custom-call(s32[5]{0:T(128)} %get-tuple-element.29.offsets_in, bf16[256,1024]{1,0:T(8,128)(2,1)} %get-tuple-element.103.q_in, bf16[256,256]{1,0:T(8,128)(2,1)} %get-tuple-element.105.k_in, ...), custom_call_target="tpu_custom_call" | custom-call | flops 1342177280 | tf_op jit(solution)/shard_map/cond/branch_0_fun/own/pallas_call | solution.py:143
  9.8 0.0 collective-permute-done.3.k_ref
  9.8 0.0 collective-permute-start.4
  9.9 0.0 collective-permute-done.v_ref
  9.9 3.0 %collective-permute-start.1 = (bf16[256,256]{1,0:T(8,128)(2,1)S(1)}, bf16[256,256]{1,0:T(8,128)(2,1)S(1)}, u32[]{:S(2)}, u32[]{:S(2)}) collective-permute-start(bf16[256,256]{1,0:T(8,128)(2,1)S(1)} %collective-permute-done.v_ref), channel_id=1, source_target_pairs={{0,8},{1,9},{2,10},{3,11},{4,12},{5,13},{6,14},{7,15},{8,0},{9,1},... | collective-permute-start | bytes 393224 | tf_op jit(solution)/shard_map/cond/branch_0_fun/ppermute | solution.py:398
  12.9 0.0 collective-permute-start.2
  12.9 0.0 collective-permute-done.6.v_ref
  12.9 0.1 attend.6
  13.1 0.0 collective-permute-done.5.k_ref
  13.1 0.0 slice-start.1
  13.1 0.2 attend.7
  13.3 0.0 collective-permute-done.4.k_ref
  13.3 0.1 last_scores.2
  13.4 2.5 %collective-permute-done.1.refs_0_ = bf16[256,256]{1,0:T(8,128)(2,1)S(1)} collective-permute-done((bf16[256,256]{1,0:T(8,128)(2,1)S(1)}, bf16[256,256]{1,0:T(8,128)(2,1)S(1)}, u32[]{:S(2)}, u32[]{:S(2)}) %collective-permute-start.1) | collective-permute-done | bytes 131104 | tf_op jit(solution)/shard_map/cond/branch_0_fun/ppermute | solution.py:398
  15.9 0.0 collective-permute-done.2.refs_1_
  15.9 0.0 slice-done
  15.9 0.0 slice-done.1
  15.9 0.8 %finish.2 = (bf16[256,1024]{1,0:T(8,128)(2,1)S(1)}, bf16[1,256,512]{2,1,0:T(8,128)(2,1)S(1)}) custom-call(bf16[256,256]{1,0:T(8,128)(2,1)S(1)} %collective-permute-done.1.refs_0_, bf16[256,256]{1,0:T(8,128)(2,1)S(1)} %collective-permute-done.2.refs_1_, bf16[8,256,256]{2,1,0:T(8,128)(2,1)S(1)} %get-tuple-element.46.refs_2_, ...), custom_call_target="tpu_custom_call" | custom-call | tf_op jit(solution)/shard_map/cond/branch_0_fun/finish/pallas_call | solution.py:282
  16.7 0.1 collective-permute-start.10
  16.8 1.0 %rest.2 = (bf16[1,256,512]{2,1,0:T(8,128)(2,1)S(1)}, bf16[1,256,1024]{2,1,0:T(8,128)(2,1)S(1)}) custom-call(bf16[256,1024]{1,0:T(8,128)(2,1)S(1)} %get-tuple-element.51.att_ref, bf16[1024,4096]{1,0:T(8,128)(2,1)S(1)} %bitcast.18), custom_call_target="tpu_custom_call" | custom-call | flops 805306368 | tf_op jit(solution)/shard_map/cond/branch_0_fun/rest/pallas_call | solution.py:305
  17.8 0.5 %collective-permute-start.7 = (bf16[1,256,1024]{2,1,0:T(8,128)(2,1)S(1)}, bf16[1,256,1024]{2,1,0:T(8,128)(2,1)S(1)}, u32[]{:S(2)}, u32[]{:S(2)}) collective-permute-start(bf16[1,256,1024]{2,1,0:T(8,128)(2,1)S(1)} %get-tuple-element.52), channel_id=1, source_target_pairs={{0,1},{1,0},{2,3},{3,2},{4,5},{5,4},{6,7},{7,6},{8,9},{9,8},{10,11... | collective-permute-start | bytes 1572872 | tf_op jit(solution)/shard_map/cond/branch_0_fun/ppermute | solution.py:359
  18.4 0.1 collective-permute-start.8
  18.4 0.0 collective-permute-done.10.refs_0_
  18.4 0.5 %sent.5 = bf16[1,256,512]{2,1,0:T(8,128)(2,1)S(1)} custom-call(bf16[256,1024]{1,0:T(8,128)(2,1)S(1)} %get-tuple-element.51.att_ref, bf16[1024,4096]{1,0:T(8,128)(2,1)S(1)} %bitcast.18, bf16[1,256,512]{2,1,0:T(8,128)(2,1)S(1)} %collective-permute-done.10.refs_0_), custom_call_target="tpu_custom_call" | custom-call | flops 268435456 | tf_op jit(solution)/shard_map/cond/branch_0_fun/sent/pallas_call | solution.py:324
  18.9 1.6 %collective-permute-start.11 = (bf16[1,256,512]{2,1,0:T(8,128)(2,1)S(1)}, bf16[1,256,512]{2,1,0:T(8,128)(2,1)S(1)}, u32[]{:S(2)}, u32[]{:S(2)}) collective-permute-start(bf16[1,256,512]{2,1,0:T(8,128)(2,1)S(1)} %sent.5), channel_id=1, source_target_pairs={{0,2},{1,3},{2,0},{3,1},{4,6},{5,7},{6,4},{7,5},{8,10},{9,11},{10,... | collective-permute-start | bytes 786440 | tf_op jit(solution)/shard_map/cond/branch_0_fun/ppermute | solution.py:359
  20.5 0.0 collective-permute-done.8.refs_0_
  20.5 0.5 %sent.4 = bf16[1,256,512]{2,1,0:T(8,128)(2,1)S(1)} custom-call(bf16[256,1024]{1,0:T(8,128)(2,1)S(1)} %get-tuple-element.51.att_ref, bf16[1024,4096]{1,0:T(8,128)(2,1)S(1)} %bitcast.18, bf16[1,256,512]{2,1,0:T(8,128)(2,1)S(1)} %collective-permute-done.8.refs_0_), custom_call_target="tpu_custom_call" | custom-call | flops 268435456 | tf_op jit(solution)/shard_map/cond/branch_0_fun/sent/pallas_call | solution.py:324
  21.0 1.4 %collective-permute-start.9 = (bf16[1,256,512]{2,1,0:T(8,128)(2,1)S(1)}, bf16[1,256,512]{2,1,0:T(8,128)(2,1)S(1)}, u32[]{:S(2)}, u32[]{:S(2)}) collective-permute-start(bf16[1,256,512]{2,1,0:T(8,128)(2,1)S(1)} %sent.4), channel_id=1, source_target_pairs={{0,2},{1,3},{2,0},{3,1},{4,6},{5,7},{6,4},{7,5},{8,10},{9,11},{10,... | collective-permute-start | bytes 786440 | tf_op jit(solution)/shard_map/cond/branch_0_fun/ppermute | solution.py:359
  22.4 0.0 collective-permute-done.7.refs_0_
  22.4 0.5 %kept.5 = f32[1,256,512]{2,1,0:T(8,128)S(1)} custom-call(bf16[256,1024]{1,0:T(8,128)(2,1)S(1)} %get-tuple-element.51.att_ref, bf16[1024,4096]{1,0:T(8,128)(2,1)S(1)} %bitcast.18, bf16[1,256,1024]{2,1,0:T(8,128)(2,1)S(1)} %collective-permute-done.7.refs_0_), custom_call_target="tpu_custom_call" | custom-call | flops 268435456 | tf_op jit(solution)/shard_map/cond/branch_0_fun/kept/pallas_call | solution.py:324
  22.8 5.3 %collective-permute-done.11 = bf16[1,256,512]{2,1,0:T(8,128)(2,1)S(1)} collective-permute-done((bf16[1,256,512]{2,1,0:T(8,128)(2,1)S(1)}, bf16[1,256,512]{2,1,0:T(8,128)(2,1)S(1)}, u32[]{:S(2)}, u32[]{:S(2)}) %collective-permute-start.11) | collective-permute-done | bytes 262176 | tf_op jit(solution)/shard_map/cond/branch_0_fun/ppermute | solution.py:359
  28.1 0.8 %output.4.refs_0_ = bf16[1024,256]{1,0:T(8,128)(2,1)} custom-call(f32[256,512]{1,0:T(8,128)S(1)} %bitcast.11, bf16[256,512]{1,0:T(8,128)(2,1)S(1)} %bitcast.13), custom_call_target="tpu_custom_call" | custom-call | tf_op jit(solution)/shard_map/cond/branch_0_fun/output/pallas_call | solution.py:346
  29.0 0.5 %kept.4 = f32[1,256,512]{2,1,0:T(8,128)S(1)} custom-call(bf16[256,1024]{1,0:T(8,128)(2,1)S(1)} %get-tuple-element.51.att_ref, bf16[1024,4096]{1,0:T(8,128)(2,1)S(1)} %bitcast.18, bf16[1,256,1024]{2,1,0:T(8,128)(2,1)S(1)} %collective-permute-done.7.refs_0_), custom_call_target="tpu_custom_call" | custom-call | flops 268435456 | tf_op jit(solution)/shard_map/cond/branch_0_fun/kept/pallas_call | solution.py:324
  29.5 3.8 %collective-permute-done.9 = bf16[1,256,512]{2,1,0:T(8,128)(2,1)S(1)} collective-permute-done((bf16[1,256,512]{2,1,0:T(8,128)(2,1)S(1)}, bf16[1,256,512]{2,1,0:T(8,128)(2,1)S(1)}, u32[]{:S(2)}, u32[]{:S(2)}) %collective-permute-start.9) | collective-permute-done | bytes 262176 | tf_op jit(solution)/shard_map/cond/branch_0_fun/ppermute | solution.py:359
  33.3 0.8 %output.5 = bf16[1024,256]{1,0:T(8,128)(2,1)} custom-call(f32[256,512]{1,0:T(8,128)S(1)} %bitcast.9, bf16[256,512]{1,0:T(8,128)(2,1)S(1)} %bitcast.14, bf16[1024,256]{1,0:T(8,128)(2,1)} %output.4.refs_0_), custom_call_target="tpu_custom_call", output_to_operand_aliasing={{}: (2, {})} | custom-call | tf_op jit(solution)/shard_map/cond/branch_0_fun/output/pallas_call | solution.py:346
  (1 shorter events, 0.0 us)
Async XLA Ops:
  0.7 9.1 %collective-permute-start.3 = (bf16[256,256]{1,0:T(8,128)(2,1)}, bf16[256,256]{1,0:T(8,128)(2,1)S(1)}, u32[]{:S(2)}, u32[]{:S(2)}) collective-permute-start(bf16[256,256]{1,0:T(8,128)(2,1)} %get-tuple-element.105.k_in), channel_id=1, source_target_pairs={{0,8},{1,9},{2,10},{3,11},{4,12},{5,13},{6,14},{7,15},{8,16},{9,17... | collective-permute-start | bytes 393224 | tf_op jit(solution)/shard_map/cond/branch_0_fun/ppermute | solution.py:398
  3.8 6.1 %collective-permute-start = (bf16[256,256]{1,0:T(8,128)(2,1)}, bf16[256,256]{1,0:T(8,128)(2,1)S(1)}, u32[]{:S(2)}, u32[]{:S(2)}) collective-permute-start(bf16[256,256]{1,0:T(8,128)(2,1)} %get-tuple-element.101.v_in), channel_id=1, source_target_pairs={{0,4},{1,5},{2,6},{3,7},{4,0},{5,1},{6,2},{7,3},{8,12},{9,13},{10,... | collective-permute-start | bytes 393224 | tf_op jit(solution)/shard_map/cond/branch_0_fun/ppermute | solution.py:398
  5.3 7.6 %collective-permute-start.6 = (bf16[256,256]{1,0:T(8,128)(2,1)}, bf16[256,256]{1,0:T(8,128)(2,1)S(1)}, u32[]{:S(2)}, u32[]{:S(2)}) collective-permute-start(bf16[256,256]{1,0:T(8,128)(2,1)} %get-tuple-element.101.v_in), channel_id=1, source_target_pairs={{0,8},{1,9},{2,10},{3,11},{4,12},{5,13},{6,14},{7,15},{8,16},{9,17... | collective-permute-start | bytes 393224 | tf_op jit(solution)/shard_map/cond/branch_0_fun/ppermute | solution.py:398
  6.9 6.2 %collective-permute-start.5 = (bf16[256,256]{1,0:T(8,128)(2,1)}, bf16[256,256]{1,0:T(8,128)(2,1)S(1)}, u32[]{:S(2)}, u32[]{:S(2)}) collective-permute-start(bf16[256,256]{1,0:T(8,128)(2,1)} %get-tuple-element.105.k_in), channel_id=1, source_target_pairs={{0,4},{1,5},{2,6},{3,7},{4,0},{5,1},{6,2},{7,3},{8,12},{9,13},{10,... | collective-permute-start | bytes 393224 | tf_op jit(solution)/shard_map/cond/branch_0_fun/ppermute | solution.py:398
  7.4 8.5 %slice-start = ((s8[8388608]{0:T(1024)(128)(4,1)}), s8[4194304]{0:T(1024)(128)(4,1)S(1)}, s32[]{:S(2)}) async-start(s8[8388608]{0:T(1024)(128)(4,1)} %bitcast.17), calls=%async_computation | async-start | bytes 8388608 | tf_op jit(solution)/shard_map/cond
  9.8 3.4 %collective-permute-start.4 = (bf16[256,256]{1,0:T(8,128)(2,1)S(1)}, bf16[256,256]{1,0:T(8,128)(2,1)S(1)}, u32[]{:S(2)}, u32[]{:S(2)}) collective-permute-start(bf16[256,256]{1,0:T(8,128)(2,1)S(1)} %collective-permute-done.3.k_ref), channel_id=1, source_target_pairs={{0,1},{1,0},{2,3},{3,2},{4,5},{5,4},{6,7},{7,6},{8,12},{9,13},{10,... | collective-permute-start | bytes 393224 | tf_op jit(solution)/shard_map/cond/branch_0_fun/ppermute | solution.py:398
  9.9 6.0 %collective-permute-start.1 = (bf16[256,256]{1,0:T(8,128)(2,1)S(1)}, bf16[256,256]{1,0:T(8,128)(2,1)S(1)}, u32[]{:S(2)}, u32[]{:S(2)}) collective-permute-start(bf16[256,256]{1,0:T(8,128)(2,1)S(1)} %collective-permute-done.v_ref), channel_id=1, source_target_pairs={{0,8},{1,9},{2,10},{3,11},{4,12},{5,13},{6,14},{7,15},{8,0},{9,1},... | collective-permute-start | bytes 393224 | tf_op jit(solution)/shard_map/cond/branch_0_fun/ppermute | solution.py:398
  12.9 2.9 %collective-permute-start.2 = (bf16[256,256]{1,0:T(8,128)(2,1)S(1)}, bf16[256,256]{1,0:T(8,128)(2,1)S(1)}, u32[]{:S(2)}, u32[]{:S(2)}) collective-permute-start(bf16[256,256]{1,0:T(8,128)(2,1)S(1)} %collective-permute-done.v_ref), channel_id=1, source_target_pairs={{0,1},{1,0},{2,3},{3,2},{4,5},{5,4},{6,7},{7,6},{8,16},{9,17},{10,... | collective-permute-start | bytes 393224 | tf_op jit(solution)/shard_map/cond/branch_0_fun/ppermute | solution.py:398
  13.1 2.8 %slice-start.1 = ((s8[8388608]{0:T(1024)(128)(4,1)}), s8[4194304]{0:T(1024)(128)(4,1)S(1)}, s32[]{:S(2)}) async-start(s8[8388608]{0:T(1024)(128)(4,1)} %bitcast.17), calls=%async_computation.1 | async-start | bytes 8388608 | tf_op jit(solution)/shard_map/cond
  16.7 1.8 %collective-permute-start.10 = (bf16[1,256,512]{2,1,0:T(8,128)(2,1)S(1)}, bf16[1,256,512]{2,1,0:T(8,128)(2,1)S(1)}, u32[]{:S(2)}, u32[]{:S(2)}) collective-permute-start(bf16[1,256,512]{2,1,0:T(8,128)(2,1)S(1)} %get-tuple-element.54), channel_id=1, source_target_pairs={{0,1},{1,0},{2,3},{3,2},{4,5},{5,4},{6,7},{7,6},{8,9},{9,8},{10,11... | collective-permute-start | bytes 786440 | tf_op jit(solution)/shard_map/cond/branch_0_fun/ppermute | solution.py:359
  17.8 4.5 %collective-permute-start.7 = (bf16[1,256,1024]{2,1,0:T(8,128)(2,1)S(1)}, bf16[1,256,1024]{2,1,0:T(8,128)(2,1)S(1)}, u32[]{:S(2)}, u32[]{:S(2)}) collective-permute-start(bf16[1,256,1024]{2,1,0:T(8,128)(2,1)S(1)} %get-tuple-element.52), channel_id=1, source_target_pairs={{0,1},{1,0},{2,3},{3,2},{4,5},{5,4},{6,7},{7,6},{8,9},{9,8},{10,11... | collective-permute-start | bytes 1572872 | tf_op jit(solution)/shard_map/cond/branch_0_fun/ppermute | solution.py:359
  18.4 2.1 %collective-permute-start.8 = (bf16[1,256,512]{2,1,0:T(8,128)(2,1)S(1)}, bf16[1,256,512]{2,1,0:T(8,128)(2,1)S(1)}, u32[]{:S(2)}, u32[]{:S(2)}) collective-permute-start(bf16[1,256,512]{2,1,0:T(8,128)(2,1)S(1)} %get-tuple-element.53), channel_id=1, source_target_pairs={{0,1},{1,0},{2,3},{3,2},{4,5},{5,4},{6,7},{7,6},{8,9},{9,8},{10,11... | collective-permute-start | bytes 786440 | tf_op jit(solution)/shard_map/cond/branch_0_fun/ppermute | solution.py:359
  18.9 9.2 %collective-permute-start.11 = (bf16[1,256,512]{2,1,0:T(8,128)(2,1)S(1)}, bf16[1,256,512]{2,1,0:T(8,128)(2,1)S(1)}, u32[]{:S(2)}, u32[]{:S(2)}) collective-permute-start(bf16[1,256,512]{2,1,0:T(8,128)(2,1)S(1)} %sent.5), channel_id=1, source_target_pairs={{0,2},{1,3},{2,0},{3,1},{4,6},{5,7},{6,4},{7,5},{8,10},{9,11},{10,... | collective-permute-start | bytes 786440 | tf_op jit(solution)/shard_map/cond/branch_0_fun/ppermute | solution.py:359
  21.0 12.3 %collective-permute-start.9 = (bf16[1,256,512]{2,1,0:T(8,128)(2,1)S(1)}, bf16[1,256,512]{2,1,0:T(8,128)(2,1)S(1)}, u32[]{:S(2)}, u32[]{:S(2)}) collective-permute-start(bf16[1,256,512]{2,1,0:T(8,128)(2,1)S(1)} %sent.4), channel_id=1, source_target_pairs={{0,2},{1,3},{2,0},{3,1},{4,6},{5,7},{6,4},{7,5},{8,10},{9,11},{10,... | collective-permute-start | bytes 786440 | tf_op jit(solution)/shard_map/cond/branch_0_fun/ppermute | solution.py:359

commit v2 on v1

--- a/solution.py
+++ b/solution.py
@@ -366,6 +366,7 @@
     *fars, near = rest_call(attended, out_weight, count)
     got_fars = [swapped(x, "head", 1) for x in (far, *fars)]
     sents = [project(got_fars[part], 0, 1, part, PARTS, jnp.bfloat16, "sent") for part in range(PARTS)]
+    near, sents[0] = lax.optimization_barrier((near, sents[0]))
     gots = [swapped(x, "head", 2) for x in sents]
     got_near = swapped(near, "head", 1)
     kepts = [project(got_near, 0, 0, part, PARTS, jnp.float32, "kept") for part in range(PARTS)]
@@ -443,7 +444,9 @@
         starts, q, state = own_call(offsets, queries, key_vectors, value_vectors)
         waiting = [(*beside, lambda x: 2 * x - 1)]
         for step in range(1, pair_steps + 1):
-            moved, state = after(shifted(moved, step), state)
+            moved = shifted(moved, step)
+            if step == 1:
+                moved, state = after(moved, state)
             waiting.insert(0 if step == 1 else 1, (*moved, lambda x, step=step: 2 * step))
             crossed = across(moved, step)
             if step < pair_steps:

time: 34.7 us -> 40.5 us (1.17)
  the two profiles are of different devices: /device:TPU:0 before, /device:TPU:20 now
where the time goes in v2:
time: 40.5 us; the launch traced here: 40.3 us
  starting transfers between devices  13.6 us (34%)
  Pallas kernels  13.3 us (33%)
  waiting for transfers between devices  12.8 us (32%)
    ppermute x10, starting transfers between devices, moved_by(): return lax.ppermute(array, ('ctx', 'head'), route)  11.9 us
    ppermute x5, waiting for transfers between devices, swapped(): lax.ppermute(array, axis, [(i, i ^ bit) for i in range(lax.axis_size(axis...  11 us
    pallas_call x4, Pallas kernels, attend_call(): pl.pallas_call(kernel, out_shape=state_shapes(width // HEAD_DIM, rows), i...  4.05 us
    pallas_call x1, Pallas kernels, own_call(): pl.pallas_call(kernel, out_shape=[jax.ShapeDtypeStruct((1, rows), jnp.int...  2.22 us
    pallas_call x4, Pallas kernels, project_call(): pl.pallas_call(kernel, out_shape=jax.ShapeDtypeStruct((count // 4, rows,...  1.9 us
    ppermute x10, waiting for transfers between devices, moved_by(): return lax.ppermute(array, ('ctx', 'head'), route)  1.76 us
    ppermute x5, starting transfers between devices, swapped(): lax.ppermute(array, axis, [(i, i ^ bit) for i in range(lax.axis_size(axis...  1.72 us
    pallas_call x2, Pallas kernels, output_call(): pl.pallas_call(kernel, out_shape=jax.ShapeDtypeStruct((size * PARTS, rows...  1.7 us
  transfers between devices with their start and end apart: 15, of which 8 were waited for; matrix products, arithmetic and copies ran while one was open for 0% of the time, Pallas kernels for 26%

profile of v2, /device:TPU:20, one launch (start us, length us, event | category | flops | bytes accessed | tf_op | source)
XLA Modules:
  0.0 40.3 jit_solution(4433838218807102280)
XLA Ops:
  0.0 0.7 %reach.1 = s32[1]{0:T(128)S(4)} custom-call(s32[5]{0:T(128)} %offsets_ref.1), custom_call_target="tpu_custom_call" | custom-call | tf_op jit(solution)/shard_map/reach/pallas_call | solution.py:111
  0.7 39.4 %conditional.1 = (bf16[1024,256]{1,0:T(8,128)(2,1)}) conditional(s32[]{:T(128)} %bitcast.8, (bf16[256,256]{1,0:T(8,128)(2,1)}, s32[5]{0:T(128)}, bf16[256,1024]{1,0:T(8,128)(2,1)}, bf16[256,256]{1,0:T(8,128)(2,1)}, bf16[1024,4096]{1,0:T(8,128)(2,1)}) %tuple.15, (bf16[256,256]{1,0:T(8,128)(2,1)}, s32[5]{0:T(128)}, bf16[256,1024]{1,0:T(8,128)(2,1)}, ...), branch_computations={%region_0.0_spmd, %region_1.0_spmd} | conditional | flops 9932111872 | bytes 36700816 | solution.py:463
  0.7 1.6 %collective-permute-start.15 = (bf16[256,256]{1,0:T(8,128)(2,1)}, bf16[256,256]{1,0:T(8,128)(2,1)S(1)}, u32[]{:S(2)}, u32[]{:S(2)}) collective-permute-start(bf16[256,256]{1,0:T(8,128)(2,1)} %get-tuple-element.106.k_in), channel_id=1, source_target_pairs={{0,8},{1,9},{2,10},{3,11},{4,12},{5,13},{6,14},{7,15},{8,16},{9,17... | collective-permute-start | bytes 393224 | tf_op jit(solution)/shard_map/cond/branch_1_fun/ppermute | solution.py:399
  2.4 0.2 collective-permute-start.12
  2.6 1.5 %collective-permute-start.20 = (bf16[256,256]{1,0:T(8,128)(2,1)}, bf16[256,256]{1,0:T(8,128)(2,1)S(1)}, u32[]{:S(2)}, u32[]{:S(2)}) collective-permute-start(bf16[256,256]{1,0:T(8,128)(2,1)} %get-tuple-element.106.k_in), channel_id=1, source_target_pairs={{0,4},{1,5},{2,6},{3,7},{4,0},{5,1},{6,2},{7,3},{8,12},{9,13},{10,... | collective-permute-start | bytes 393224 | tf_op jit(solution)/shard_map/cond/branch_1_fun/ppermute | solution.py:399
  4.1 0.5 %collective-permute-start.21 = (bf16[256,256]{1,0:T(8,128)(2,1)}, bf16[256,256]{1,0:T(8,128)(2,1)S(1)}, u32[]{:S(2)}, u32[]{:S(2)}) collective-permute-start(bf16[256,256]{1,0:T(8,128)(2,1)} %get-tuple-element.102.v_in), channel_id=1, source_target_pairs={{0,4},{1,5},{2,6},{3,7},{4,0},{5,1},{6,2},{7,3},{8,12},{9,13},{10,... | collective-permute-start | bytes 393224 | tf_op jit(solution)/shard_map/cond/branch_1_fun/ppermute | solution.py:399
  4.6 2.2 %own.3 = (s32[1,256]{1,0:T(1,128)S(1)}, bf16[256,1024]{1,0:T(8,128)(2,1)S(1)}, f32[8,256]{1,0:T(8,128)S(1)}, f32[8,256]{1,0:T(8,128)S(1)}, f32[8,128,256]{2,1,0:T(8,128)S(1)}) custom-call(s32[5]{0:T(128)} %get-tuple-element.58.offsets_in, bf16[256,1024]{1,0:T(8,128)(2,1)} %get-tuple-element.104.q_in, bf16[256,256]{1,0:T(8,128)(2,1)} %get-tuple-element.106.k_in, ...), custom_call_target="tpu_custom_call" | custom-call | flops 1342177280 | tf_op jit(solution)/shard_map/cond/branch_1_fun/own/pallas_call | solution.py:143
  6.9 0.5 %collective-permute-done.15.k_ref = bf16[256,256]{1,0:T(8,128)(2,1)S(1)} collective-permute-done((bf16[256,256]{1,0:T(8,128)(2,1)}, bf16[256,256]{1,0:T(8,128)(2,1)S(1)}, u32[]{:S(2)}, u32[]{:S(2)}) %collective-permute-start.15) | collective-permute-done | bytes 131104 | tf_op jit(solution)/shard_map/cond/branch_1_fun/ppermute | solution.py:399
  7.4 1.5 %collective-permute-start.18 = (bf16[256,256]{1,0:T(8,128)(2,1)S(1)}, bf16[256,256]{1,0:T(8,128)(2,1)S(1)}, u32[]{:S(2)}, u32[]{:S(2)}) collective-permute-start(bf16[256,256]{1,0:T(8,128)(2,1)S(1)} %collective-permute-done.15.k_ref), channel_id=1, source_target_pairs={{0,1},{1,0},{2,3},{3,2},{4,5},{5,4},{6,7},{7,6},{8,12},{9,13},{10,... | collective-permute-start | bytes 393224 | tf_op jit(solution)/shard_map/cond/branch_1_fun/ppermute | solution.py:399
  8.9 1.6 %collective-permute-start.16 = (bf16[256,256]{1,0:T(8,128)(2,1)S(1)}, bf16[256,256]{1,0:T(8,128)(2,1)S(1)}, u32[]{:S(2)}, u32[]{:S(2)}) collective-permute-start(bf16[256,256]{1,0:T(8,128)(2,1)S(1)} %collective-permute-done.15.k_ref), channel_id=1, source_target_pairs={{0,1},{1,0},{2,3},{3,2},{4,5},{5,4},{6,7},{7,6},{8,16},{9,17},{10,... | collective-permute-start | bytes 393224 | tf_op jit(solution)/shard_map/cond/branch_1_fun/ppermute | solution.py:399
  10.5 0.0 collective-permute-done.12.v_ref
  10.5 0.5 %collective-permute-start.19 = (bf16[256,256]{1,0:T(8,128)(2,1)S(1)}, bf16[256,256]{1,0:T(8,128)(2,1)S(1)}, u32[]{:S(2)}, u32[]{:S(2)}) collective-permute-start(bf16[256,256]{1,0:T(8,128)(2,1)S(1)} %collective-permute-done.12.v_ref), channel_id=1, source_target_pairs={{0,1},{1,0},{2,3},{3,2},{4,5},{5,4},{6,7},{7,6},{8,12},{9,13},{10,... | collective-permute-start | bytes 393224 | tf_op jit(solution)/shard_map/cond/branch_1_fun/ppermute | solution.py:399
  11.0 0.0 collective-permute-done.20.k_ref
  11.0 1.6 %collective-permute-start.13 = (bf16[256,256]{1,0:T(8,128)(2,1)S(1)}, bf16[256,256]{1,0:T(8,128)(2,1)S(1)}, u32[]{:S(2)}, u32[]{:S(2)}) collective-permute-start(bf16[256,256]{1,0:T(8,128)(2,1)S(1)} %collective-permute-done.12.v_ref), channel_id=1, source_target_pairs={{0,1},{1,0},{2,3},{3,2},{4,5},{5,4},{6,7},{7,6},{8,16},{9,17},{10,... | collective-permute-start | bytes 393224 | tf_op jit(solution)/shard_map/cond/branch_1_fun/ppermute | solution.py:399
  12.6 1.2 %attend.8 = (f32[8,256]{1,0:T(8,128)S(1)}, f32[8,256]{1,0:T(8,128)S(1)}, f32[8,128,256]{2,1,0:T(8,128)S(1)}) custom-call(s32[1,256]{1,0:T(1,128)S(1)} %get-tuple-element.61.starts_ref, bf16[256,1024]{1,0:T(8,128)(2,1)S(1)} %get-tuple-element.62.q_ref, ...), custom_call_target="tpu_custom_call", output_to_operand_aliasing={{0}: (4, {}), {1}: (5, {}), {2}: (6, {})} | custom-call | flops 1342177280 | tf_op jit(solution)/shard_map/cond/branch_1_fun/attend/pallas_call | solution.py:195
  13.8 0.0 collective-permute-done.21.v_ref
  13.9 0.0 slice-start.2
  13.9 0.3 attend.9
  14.2 0.4 %collective-permute-done.16.k_ref = bf16[256,256]{1,0:T(8,128)(2,1)S(1)} collective-permute-done((bf16[256,256]{1,0:T(8,128)(2,1)S(1)}, bf16[256,256]{1,0:T(8,128)(2,1)S(1)}, u32[]{:S(2)}, u32[]{:S(2)}) %collective-permute-start.16) | collective-permute-done | bytes 131104 | tf_op jit(solution)/shard_map/cond/branch_1_fun/ppermute | solution.py:399
  14.6 1.9 %collective-permute-start.17 = (bf16[256,256]{1,0:T(8,128)(2,1)S(1)}, bf16[256,256]{1,0:T(8,128)(2,1)S(1)}, u32[]{:S(2)}, u32[]{:S(2)}) collective-permute-start(bf16[256,256]{1,0:T(8,128)(2,1)S(1)} %collective-permute-done.16.k_ref), channel_id=1, source_target_pairs={{0,1},{1,0},{2,3},{3,2},{4,5},{5,4},{6,7},{7,6},{8,9},{9,8},{10,11... | collective-permute-start | bytes 393224 | tf_op jit(solution)/shard_map/cond/branch_1_fun/ppermute | solution.py:399
  16.5 0.0 collective-permute-done.13.v_ref
  16.5 1.0 %collective-permute-start.14 = (bf16[256,256]{1,0:T(8,128)(2,1)S(1)}, bf16[256,256]{1,0:T(8,128)(2,1)S(1)}, u32[]{:S(2)}, u32[]{:S(2)}) collective-permute-start(bf16[256,256]{1,0:T(8,128)(2,1)S(1)} %collective-permute-done.13.v_ref), channel_id=1, source_target_pairs={{0,1},{1,0},{2,3},{3,2},{4,5},{5,4},{6,7},{7,6},{8,9},{9,8},{10,11... | collective-permute-start | bytes 393224 | tf_op jit(solution)/shard_map/cond/branch_1_fun/ppermute | solution.py:399
  17.5 0.0 collective-permute-done.18.k_ref
  17.5 0.0 collective-permute-done.19.v_ref
  17.5 1.2 %attend.10 = (f32[8,256]{1,0:T(8,128)S(1)}, f32[8,256]{1,0:T(8,128)S(1)}, f32[8,128,256]{2,1,0:T(8,128)S(1)}) custom-call(s32[1,256]{1,0:T(1,128)S(1)} %get-tuple-element.61.starts_ref, bf16[256,1024]{1,0:T(8,128)(2,1)S(1)} %get-tuple-element.62.q_ref, ...), custom_call_target="tpu_custom_call", output_to_operand_aliasing={{0}: (4, {}), {1}: (5, {}), {2}: (6, {})} | custom-call | flops 1342177280 | tf_op jit(solution)/shard_map/cond/branch_1_fun/attend/pallas_call | solution.py:195
  18.7 0.0 slice-start.3
  18.7 1.3 %attend.11 = (f32[8,256]{1,0:T(8,128)S(1)}, f32[8,256]{1,0:T(8,128)S(1)}, f32[8,128,256]{2,1,0:T(8,128)S(1)}) custom-call(s32[1,256]{1,0:T(1,128)S(1)} %get-tuple-element.61.starts_ref, bf16[256,1024]{1,0:T(8,128)(2,1)S(1)} %get-tuple-element.62.q_ref, ...), custom_call_target="tpu_custom_call", output_to_operand_aliasing={{0}: (4, {}), {1}: (5, {}), {2}: (6, {})} | custom-call | flops 1342177280 | tf_op jit(solution)/shard_map/cond/branch_1_fun/attend/pallas_call | solution.py:195
  20.0 0.3 collective-permute-done.17.k_ref
  20.2 0.9 %last_scores.3 = (f32[8,256]{1,0:T(8,128)S(1)}, f32[8,256]{1,0:T(8,128)S(1)}, bf16[8,256,256]{2,1,0:T(8,128)(2,1)S(1)}) custom-call(s32[1,256]{1,0:T(1,128)S(1)} %get-tuple-element.61.starts_ref, bf16[256,1024]{1,0:T(8,128)(2,1)S(1)} %get-tuple-element.62.q_ref, bf16[256,256]{1,0:T(8,128)(2,1)S(1)} %collective-permute-done.17.k_ref, ...), custom_call_target="tpu_custom_call" | custom-call | flops 1342177280 | tf_op jit(solution)/shard_map/cond/branch_1_fun/last_scores/pallas_call | solution.py:229
  21.1 0.5 %collective-permute-done.14.refs_0_ = bf16[256,256]{1,0:T(8,128)(2,1)S(1)} collective-permute-done((bf16[256,256]{1,0:T(8,128)(2,1)S(1)}, bf16[256,256]{1,0:T(8,128)(2,1)S(1)}, u32[]{:S(2)}, u32[]{:S(2)}) %collective-permute-start.14) | collective-permute-done | bytes 131104 | tf_op jit(solution)/shard_map/cond/branch_1_fun/ppermute | solution.py:399
  21.7 0.8 %finish.3 = (bf16[256,1024]{1,0:T(8,128)(2,1)S(1)}, bf16[1,256,512]{2,1,0:T(8,128)(2,1)S(1)}) custom-call(bf16[256,256]{1,0:T(8,128)(2,1)S(1)} %collective-permute-done.14.refs_0_, bf16[8,256,256]{2,1,0:T(8,128)(2,1)S(1)} %get-tuple-element.81.refs_1_, f32[8,256]{1,0:T(8,128)S(1)} %get-tuple-element.82.refs_2_, f32[8,256]{1,0:T(8,128)S(1)} %get-tuple-element.83.refs_3_, ...), custom_call_target="tpu_custom_call" | custom-call | tf_op jit(solution)/shard_map/cond/branch_1_fun/finish/pallas_call | solution.py:282
  22.4 0.1 collective-permute-start.22
  22.5 1.0 %rest.3 = (bf16[1,256,512]{2,1,0:T(8,128)(2,1)S(1)}, bf16[1,256,1024]{2,1,0:T(8,128)(2,1)S(1)}) custom-call(bf16[256,1024]{1,0:T(8,128)(2,1)S(1)} %get-tuple-element.86.att_ref, bf16[1024,4096]{1,0:T(8,128)(2,1)S(1)} %bitcast.20), custom_call_target="tpu_custom_call" | custom-call | flops 805306368 | tf_op jit(solution)/shard_map/cond/branch_1_fun/rest/pallas_call | solution.py:305
  23.6 0.5 %collective-permute-done.22.refs_0_ = bf16[1,256,512]{2,1,0:T(8,128)(2,1)S(1)} collective-permute-done((bf16[1,256,512]{2,1,0:T(8,128)(2,1)S(1)}, bf16[1,256,512]{2,1,0:T(8,128)(2,1)S(1)}, u32[]{:S(2)}, u32[]{:S(2)}) %collective-permute-start.22) | collective-permute-done | bytes 262176 | tf_op jit(solution)/shard_map/cond/branch_1_fun/ppermute | solution.py:359
  24.0 0.5 %sent.6 = bf16[1,256,512]{2,1,0:T(8,128)(2,1)S(1)} custom-call(bf16[256,1024]{1,0:T(8,128)(2,1)S(1)} %get-tuple-element.86.att_ref, bf16[1024,4096]{1,0:T(8,128)(2,1)S(1)} %bitcast.20, bf16[1,256,512]{2,1,0:T(8,128)(2,1)S(1)} %collective-permute-done.22.refs_0_), custom_call_target="tpu_custom_call" | custom-call | flops 268435456 | tf_op jit(solution)/shard_map/cond/branch_1_fun/sent/pallas_call | solution.py:324
  24.5 0.2 collective-permute-start.23
  24.7 0.4 collective-permute-start.24
  25.1 0.5 %collective-permute-start.26 = (bf16[1,256,512]{2,1,0:T(8,128)(2,1)S(1)}, bf16[1,256,512]{2,1,0:T(8,128)(2,1)S(1)}, u32[]{:S(2)}, u32[]{:S(2)}) collective-permute-start(bf16[1,256,512]{2,1,0:T(8,128)(2,1)S(1)} %sent.6), channel_id=1, source_target_pairs={{0,2},{1,3},{2,0},{3,1},{4,6},{5,7},{6,4},{7,5},{8,10},{9,11},{10,... | collective-permute-start | bytes 786440 | tf_op jit(solution)/shard_map/cond/branch_1_fun/ppermute | solution.py:359
  25.6 1.3 %collective-permute-done.24.refs_0_ = bf16[1,256,512]{2,1,0:T(8,128)(2,1)S(1)} collective-permute-done((bf16[1,256,512]{2,1,0:T(8,128)(2,1)S(1)}, bf16[1,256,512]{2,1,0:T(8,128)(2,1)S(1)}, u32[]{:S(2)}, u32[]{:S(2)}) %collective-permute-start.24) | collective-permute-done | bytes 262176 | tf_op jit(solution)/shard_map/cond/branch_1_fun/ppermute | solution.py:359
  26.9 0.5 %sent.7 = bf16[1,256,512]{2,1,0:T(8,128)(2,1)S(1)} custom-call(bf16[256,1024]{1,0:T(8,128)(2,1)S(1)} %get-tuple-element.86.att_ref, bf16[1024,4096]{1,0:T(8,128)(2,1)S(1)} %bitcast.20, bf16[1,256,512]{2,1,0:T(8,128)(2,1)S(1)} %collective-permute-done.24.refs_0_), custom_call_target="tpu_custom_call" | custom-call | flops 268435456 | tf_op jit(solution)/shard_map/cond/branch_1_fun/sent/pallas_call | solution.py:324
  27.3 0.6 %collective-permute-start.25 = (bf16[1,256,512]{2,1,0:T(8,128)(2,1)S(1)}, bf16[1,256,512]{2,1,0:T(8,128)(2,1)S(1)}, u32[]{:S(2)}, u32[]{:S(2)}) collective-permute-start(bf16[1,256,512]{2,1,0:T(8,128)(2,1)S(1)} %sent.7), channel_id=1, source_target_pairs={{0,2},{1,3},{2,0},{3,1},{4,6},{5,7},{6,4},{7,5},{8,10},{9,11},{10,... | collective-permute-start | bytes 786440 | tf_op jit(solution)/shard_map/cond/branch_1_fun/ppermute | solution.py:359
  27.9 0.0 collective-permute-done.23.refs_0_
  27.9 0.5 %kept.7 = f32[1,256,512]{2,1,0:T(8,128)S(1)} custom-call(bf16[256,1024]{1,0:T(8,128)(2,1)S(1)} %get-tuple-element.86.att_ref, bf16[1024,4096]{1,0:T(8,128)(2,1)S(1)} %bitcast.20, bf16[1,256,1024]{2,1,0:T(8,128)(2,1)S(1)} %collective-permute-done.23.refs_0_), custom_call_target="tpu_custom_call" | custom-call | flops 268435456 | tf_op jit(solution)/shard_map/cond/branch_1_fun/kept/pallas_call | solution.py:324
  28.4 5.9 %collective-permute-done.26 = bf16[1,256,512]{2,1,0:T(8,128)(2,1)S(1)} collective-permute-done((bf16[1,256,512]{2,1,0:T(8,128)(2,1)S(1)}, bf16[1,256,512]{2,1,0:T(8,128)(2,1)S(1)}, u32[]{:S(2)}, u32[]{:S(2)}) %collective-permute-start.26) | collective-permute-done | bytes 262176 | tf_op jit(solution)/shard_map/cond/branch_1_fun/ppermute | solution.py:359
  34.2 0.8 %output.6.refs_0_ = bf16[1024,256]{1,0:T(8,128)(2,1)} custom-call(f32[256,512]{1,0:T(8,128)S(1)} %bitcast.12, bf16[256,512]{1,0:T(8,128)(2,1)S(1)} %bitcast.15), custom_call_target="tpu_custom_call" | custom-call | tf_op jit(solution)/shard_map/cond/branch_1_fun/output/pallas_call | solution.py:346
  35.1 0.5 %kept.6 = f32[1,256,512]{2,1,0:T(8,128)S(1)} custom-call(bf16[256,1024]{1,0:T(8,128)(2,1)S(1)} %get-tuple-element.86.att_ref, bf16[1024,4096]{1,0:T(8,128)(2,1)S(1)} %bitcast.20, bf16[1,256,1024]{2,1,0:T(8,128)(2,1)S(1)} %collective-permute-done.23.refs_0_), custom_call_target="tpu_custom_call" | custom-call | flops 268435456 | tf_op jit(solution)/shard_map/cond/branch_1_fun/kept/pallas_call | solution.py:324
  35.6 3.5 %collective-permute-done.25 = bf16[1,256,512]{2,1,0:T(8,128)(2,1)S(1)} collective-permute-done((bf16[1,256,512]{2,1,0:T(8,128)(2,1)S(1)}, bf16[1,256,512]{2,1,0:T(8,128)(2,1)S(1)}, u32[]{:S(2)}, u32[]{:S(2)}) %collective-permute-start.25) | collective-permute-done | bytes 262176 | tf_op jit(solution)/shard_map/cond/branch_1_fun/ppermute | solution.py:359
  39.0 0.8 %output.7 = bf16[1024,256]{1,0:T(8,128)(2,1)} custom-call(f32[256,512]{1,0:T(8,128)S(1)} %bitcast.10, bf16[256,512]{1,0:T(8,128)(2,1)S(1)} %bitcast.16, bf16[1024,256]{1,0:T(8,128)(2,1)} %output.6.refs_0_), custom_call_target="tpu_custom_call", output_to_operand_aliasing={{}: (2, {})} | custom-call | tf_op jit(solution)/shard_map/cond/branch_1_fun/output/pallas_call | solution.py:346
  (3 shorter events, 0.0 us)
Async XLA Ops:
  0.7 6.6 %collective-permute-start.15 = (bf16[256,256]{1,0:T(8,128)(2,1)}, bf16[256,256]{1,0:T(8,128)(2,1)S(1)}, u32[]{:S(2)}, u32[]{:S(2)}) collective-permute-start(bf16[256,256]{1,0:T(8,128)(2,1)} %get-tuple-element.106.k_in), channel_id=1, source_target_pairs={{0,8},{1,9},{2,10},{3,11},{4,12},{5,13},{6,14},{7,15},{8,16},{9,17... | collective-permute-start | bytes 393224 | tf_op jit(solution)/shard_map/cond/branch_1_fun/ppermute | solution.py:399
  2.4 8.1 %collective-permute-start.12 = (bf16[256,256]{1,0:T(8,128)(2,1)}, bf16[256,256]{1,0:T(8,128)(2,1)S(1)}, u32[]{:S(2)}, u32[]{:S(2)}) collective-permute-start(bf16[256,256]{1,0:T(8,128)(2,1)} %get-tuple-element.102.v_in), channel_id=1, source_target_pairs={{0,8},{1,9},{2,10},{3,11},{4,12},{5,13},{6,14},{7,15},{8,16},{9,17... | collective-permute-start | bytes 393224 | tf_op jit(solution)/shard_map/cond/branch_1_fun/ppermute | solution.py:399
  2.6 8.4 %collective-permute-start.20 = (bf16[256,256]{1,0:T(8,128)(2,1)}, bf16[256,256]{1,0:T(8,128)(2,1)S(1)}, u32[]{:S(2)}, u32[]{:S(2)}) collective-permute-start(bf16[256,256]{1,0:T(8,128)(2,1)} %get-tuple-element.106.k_in), channel_id=1, source_target_pairs={{0,4},{1,5},{2,6},{3,7},{4,0},{5,1},{6,2},{7,3},{8,12},{9,13},{10,... | collective-permute-start | bytes 393224 | tf_op jit(solution)/shard_map/cond/branch_1_fun/ppermute | solution.py:399
  4.1 9.8 %collective-permute-start.21 = (bf16[256,256]{1,0:T(8,128)(2,1)}, bf16[256,256]{1,0:T(8,128)(2,1)S(1)}, u32[]{:S(2)}, u32[]{:S(2)}) collective-permute-start(bf16[256,256]{1,0:T(8,128)(2,1)} %get-tuple-element.102.v_in), channel_id=1, source_target_pairs={{0,4},{1,5},{2,6},{3,7},{4,0},{5,1},{6,2},{7,3},{8,12},{9,13},{10,... | collective-permute-start | bytes 393224 | tf_op jit(solution)/shard_map/cond/branch_1_fun/ppermute | solution.py:399
  7.4 10.1 %collective-permute-start.18 = (bf16[256,256]{1,0:T(8,128)(2,1)S(1)}, bf16[256,256]{1,0:T(8,128)(2,1)S(1)}, u32[]{:S(2)}, u32[]{:S(2)}) collective-permute-start(bf16[256,256]{1,0:T(8,128)(2,1)S(1)} %collective-permute-done.15.k_ref), channel_id=1, source_target_pairs={{0,1},{1,0},{2,3},{3,2},{4,5},{5,4},{6,7},{7,6},{8,12},{9,13},{10,... | collective-permute-start | bytes 393224 | tf_op jit(solution)/shard_map/cond/branch_1_fun/ppermute | solution.py:399
  8.9 5.8 %collective-permute-start.16 = (bf16[256,256]{1,0:T(8,128)(2,1)S(1)}, bf16[256,256]{1,0:T(8,128)(2,1)S(1)}, u32[]{:S(2)}, u32[]{:S(2)}) collective-permute-start(bf16[256,256]{1,0:T(8,128)(2,1)S(1)} %collective-permute-done.15.k_ref), channel_id=1, source_target_pairs={{0,1},{1,0},{2,3},{3,2},{4,5},{5,4},{6,7},{7,6},{8,16},{9,17},{10,... | collective-permute-start | bytes 393224 | tf_op jit(solution)/shard_map/cond/branch_1_fun/ppermute | solution.py:399
  10.5 7.0 %collective-permute-start.19 = (bf16[256,256]{1,0:T(8,128)(2,1)S(1)}, bf16[256,256]{1,0:T(8,128)(2,1)S(1)}, u32[]{:S(2)}, u32[]{:S(2)}) collective-permute-start(bf16[256,256]{1,0:T(8,128)(2,1)S(1)} %collective-permute-done.12.v_ref), channel_id=1, source_target_pairs={{0,1},{1,0},{2,3},{3,2},{4,5},{5,4},{6,7},{7,6},{8,12},{9,13},{10,... | collective-permute-start | bytes 393224 | tf_op jit(solution)/shard_map/cond/branch_1_fun/ppermute | solution.py:399
  11.0 5.5 %collective-permute-start.13 = (bf16[256,256]{1,0:T(8,128)(2,1)S(1)}, bf16[256,256]{1,0:T(8,128)(2,1)S(1)}, u32[]{:S(2)}, u32[]{:S(2)}) collective-permute-start(bf16[256,256]{1,0:T(8,128)(2,1)S(1)} %collective-permute-done.12.v_ref), channel_id=1, source_target_pairs={{0,1},{1,0},{2,3},{3,2},{4,5},{5,4},{6,7},{7,6},{8,16},{9,17},{10,... | collective-permute-start | bytes 393224 | tf_op jit(solution)/shard_map/cond/branch_1_fun/ppermute | solution.py:399
  13.9 7.8 %slice-start.2 = ((s8[8388608]{0:T(1024)(128)(4,1)}), s8[4194304]{0:T(1024)(128)(4,1)S(1)}, s32[]{:S(2)}) async-start(s8[8388608]{0:T(1024)(128)(4,1)} %bitcast.19), calls=%async_computation.2 | async-start | bytes 8388608 | tf_op jit(solution)/shard_map/cond
  14.6 5.6 %collective-permute-start.17 = (bf16[256,256]{1,0:T(8,128)(2,1)S(1)}, bf16[256,256]{1,0:T(8,128)(2,1)S(1)}, u32[]{:S(2)}, u32[]{:S(2)}) collective-permute-start(bf16[256,256]{1,0:T(8,128)(2,1)S(1)} %collective-permute-done.16.k_ref), channel_id=1, source_target_pairs={{0,1},{1,0},{2,3},{3,2},{4,5},{5,4},{6,7},{7,6},{8,9},{9,8},{10,11... | collective-permute-start | bytes 393224 | tf_op jit(solution)/shard_map/cond/branch_1_fun/ppermute | solution.py:399
  16.5 5.1 %collective-permute-start.14 = (bf16[256,256]{1,0:T(8,128)(2,1)S(1)}, bf16[256,256]{1,0:T(8,128)(2,1)S(1)}, u32[]{:S(2)}, u32[]{:S(2)}) collective-permute-start(bf16[256,256]{1,0:T(8,128)(2,1)S(1)} %collective-permute-done.13.v_ref), channel_id=1, source_target_pairs={{0,1},{1,0},{2,3},{3,2},{4,5},{5,4},{6,7},{7,6},{8,9},{9,8},{10,11... | collective-permute-start | bytes 393224 | tf_op jit(solution)/shard_map/cond/branch_1_fun/ppermute | solution.py:399
  18.7 3.0 %slice-start.3 = ((s8[8388608]{0:T(1024)(128)(4,1)}), s8[4194304]{0:T(1024)(128)(4,1)S(1)}, s32[]{:S(2)}) async-start(s8[8388608]{0:T(1024)(128)(4,1)} %bitcast.19), calls=%async_computation.3 | async-start | bytes 8388608 | tf_op jit(solution)/shard_map/cond
  22.4 1.6 %collective-permute-start.22 = (bf16[1,256,512]{2,1,0:T(8,128)(2,1)S(1)}, bf16[1,256,512]{2,1,0:T(8,128)(2,1)S(1)}, u32[]{:S(2)}, u32[]{:S(2)}) collective-permute-start(bf16[1,256,512]{2,1,0:T(8,128)(2,1)S(1)} %get-tuple-element.88), channel_id=1, source_target_pairs={{0,1},{1,0},{2,3},{3,2},{4,5},{5,4},{6,7},{7,6},{8,9},{9,8},{10,11... | collective-permute-start | bytes 786440 | tf_op jit(solution)/shard_map/cond/branch_1_fun/ppermute | solution.py:359
  24.5 3.4 %collective-permute-start.23 = (bf16[1,256,1024]{2,1,0:T(8,128)(2,1)S(1)}, bf16[1,256,1024]{2,1,0:T(8,128)(2,1)S(1)}, u32[]{:S(2)}, u32[]{:S(2)}) collective-permute-start(bf16[1,256,1024]{2,1,0:T(8,128)(2,1)S(1)} %get-tuple-element.89), channel_id=1, source_target_pairs={{0,1},{1,0},{2,3},{3,2},{4,5},{5,4},{6,7},{7,6},{8,9},{9,8},{10,11... | collective-permute-start | bytes 1572872 | tf_op jit(solution)/shard_map/cond/branch_1_fun/ppermute | solution.py:359
  24.7 2.1 %collective-permute-start.24 = (bf16[1,256,512]{2,1,0:T(8,128)(2,1)S(1)}, bf16[1,256,512]{2,1,0:T(8,128)(2,1)S(1)}, u32[]{:S(2)}, u32[]{:S(2)}) collective-permute-start(bf16[1,256,512]{2,1,0:T(8,128)(2,1)S(1)} %get-tuple-element.90), channel_id=1, source_target_pairs={{0,1},{1,0},{2,3},{3,2},{4,5},{5,4},{6,7},{7,6},{8,9},{9,8},{10,11... | collective-permute-start | bytes 786440 | tf_op jit(solution)/shard_map/cond/branch_1_fun/ppermute | solution.py:359
  25.1 9.2 %collective-permute-start.26 = (bf16[1,256,512]{2,1,0:T(8,128)(2,1)S(1)}, bf16[1,256,512]{2,1,0:T(8,128)(2,1)S(1)}, u32[]{:S(2)}, u32[]{:S(2)}) collective-permute-start(bf16[1,256,512]{2,1,0:T(8,128)(2,1)S(1)} %sent.6), channel_id=1, source_target_pairs={{0,2},{1,3},{2,0},{3,1},{4,6},{5,7},{6,4},{7,5},{8,10},{9,11},{10,... | collective-permute-start | bytes 786440 | tf_op jit(solution)/shard_map/cond/branch_1_fun/ppermute | solution.py:359
  27.3 11.7 %collective-permute-start.25 = (bf16[1,256,512]{2,1,0:T(8,128)(2,1)S(1)}, bf16[1,256,512]{2,1,0:T(8,128)(2,1)S(1)}, u32[]{:S(2)}, u32[]{:S(2)}) collective-permute-start(bf16[1,256,512]{2,1,0:T(8,128)(2,1)S(1)} %sent.7), channel_id=1, source_target_pairs={{0,2},{1,3},{2,0},{3,1},{4,6},{5,7},{6,4},{7,5},{8,10},{9,11},{10,... | collective-permute-start | bytes 786440 | tf_op jit(solution)/shard_map/cond/branch_1_fun/ppermute | solution.py:359

commit v3 on v2

--- a/solution.py
+++ b/solution.py
@@ -132,9 +132,10 @@
         starts = document_starts(offsets_ref, first, rows)
         starts_ref[...] = starts
         visible = visible_keys(starts, first, rows, first)
-        for copy in copies[1:]:
+        for copy in copies[1:3]:
             copy.wait()
         tops, totals, weights, _ = score_block(q_ref, k_ref, visible, None)
+        copies[3].wait()
         store_rows(top_ref, tops)
         store_rows(total_ref, totals)
         for h, out in enumerate(value_block(v_ref, weights, None, None)):

time: 40.5 us -> 34.8 us (0.86)
  the two profiles are of different devices: /device:TPU:20 before, /device:TPU:0 now
where the time goes in v3:
time: 34.8 us; the launch traced here: 34.6 us
  starting transfers between devices  13.5 us (39%)
  waiting for transfers between devices  11.5 us (33%)
  Pallas kernels  8.97 us (26%)
  loops' own time  0.4 us (1%)
    ppermute x7, starting transfers between devices, moved_by(): return lax.ppermute(array, ('ctx', 'head'), route)  9.79 us
    ppermute x5, waiting for transfers between devices, swapped(): lax.ppermute(array, axis, [(i, i ^ bit) for i in range(lax.axis_size(axis...  9.02 us
    ppermute x5, starting transfers between devices, swapped(): lax.ppermute(array, axis, [(i, i ^ bit) for i in range(lax.axis_size(axis...  3.75 us
    ppermute x7, waiting for transfers between devices, moved_by(): return lax.ppermute(array, ('ctx', 'head'), route)  2.51 us
    pallas_call x1, Pallas kernels, own_call(): pl.pallas_call(kernel, out_shape=[jax.ShapeDtypeStruct((1, rows), jnp.int...  2.45 us
    pallas_call x4, Pallas kernels, project_call(): pl.pallas_call(kernel, out_shape=jax.ShapeDtypeStruct((count // 4, rows,...  1.9 us
    pallas_call x2, Pallas kernels, output_call(): pl.pallas_call(kernel, out_shape=jax.ShapeDtypeStruct((size * PARTS, rows...  1.7 us
    pallas_call x1, Pallas kernels, rest_call(): pl.pallas_call(kernel, out_shape=[jax.ShapeDtypeStruct((count // 4, rows,...  1.04 us
  transfers between devices with their start and end apart: 12, of which 5 were waited for; matrix products, arithmetic and copies ran while one was open for 0% of the time, Pallas kernels for 18%

profile of v3, /device:TPU:0, one launch (start us, length us, event | category | flops | bytes accessed | tf_op | source)
XLA Modules:
  0.0 34.6 jit_solution(4066955522200982057)
XLA Ops:
  0.0 0.7 %reach.1 = s32[1]{0:T(128)S(4)} custom-call(s32[5]{0:T(128)} %offsets_ref.1), custom_call_target="tpu_custom_call" | custom-call | tf_op jit(solution)/shard_map/reach/pallas_call | solution.py:111
  0.7 33.7 %conditional.1 = (bf16[1024,256]{1,0:T(8,128)(2,1)}) conditional(s32[]{:T(128)} %bitcast.8, (bf16[256,256]{1,0:T(8,128)(2,1)}, s32[5]{0:T(128)}, bf16[256,1024]{1,0:T(8,128)(2,1)}, bf16[256,256]{1,0:T(8,128)(2,1)}, bf16[1024,4096]{1,0:T(8,128)(2,1)}) %tuple.15, (bf16[256,256]{1,0:T(8,128)(2,1)}, s32[5]{0:T(128)}, bf16[256,1024]{1,0:T(8,128)(2,1)}, ...), branch_computations={%region_0.0_spmd, %region_1.0_spmd} | conditional | flops 9932111872 | bytes 36700816 | solution.py:464
  0.7 3.1 %collective-permute-start.3 = (bf16[256,256]{1,0:T(8,128)(2,1)}, bf16[256,256]{1,0:T(8,128)(2,1)S(1)}, u32[]{:S(2)}, u32[]{:S(2)}) collective-permute-start(bf16[256,256]{1,0:T(8,128)(2,1)} %get-tuple-element.105.k_in), channel_id=1, source_target_pairs={{0,8},{1,9},{2,10},{3,11},{4,12},{5,13},{6,14},{7,15},{8,16},{9,17... | collective-permute-start | bytes 393224 | tf_op jit(solution)/shard_map/cond/branch_0_fun/ppermute | solution.py:400
  3.8 1.5 %collective-permute-start = (bf16[256,256]{1,0:T(8,128)(2,1)}, bf16[256,256]{1,0:T(8,128)(2,1)S(1)}, u32[]{:S(2)}, u32[]{:S(2)}) collective-permute-start(bf16[256,256]{1,0:T(8,128)(2,1)} %get-tuple-element.101.v_in), channel_id=1, source_target_pairs={{0,4},{1,5},{2,6},{3,7},{4,0},{5,1},{6,2},{7,3},{8,12},{9,13},{10,... | collective-permute-start | bytes 393224 | tf_op jit(solution)/shard_map/cond/branch_0_fun/ppermute | solution.py:400
  5.3 1.6 %collective-permute-start.6 = (bf16[256,256]{1,0:T(8,128)(2,1)}, bf16[256,256]{1,0:T(8,128)(2,1)S(1)}, u32[]{:S(2)}, u32[]{:S(2)}) collective-permute-start(bf16[256,256]{1,0:T(8,128)(2,1)} %get-tuple-element.101.v_in), channel_id=1, source_target_pairs={{0,8},{1,9},{2,10},{3,11},{4,12},{5,13},{6,14},{7,15},{8,16},{9,17... | collective-permute-start | bytes 393224 | tf_op jit(solution)/shard_map/cond/branch_0_fun/ppermute | solution.py:400
  6.9 0.5 %collective-permute-start.5 = (bf16[256,256]{1,0:T(8,128)(2,1)}, bf16[256,256]{1,0:T(8,128)(2,1)S(1)}, u32[]{:S(2)}, u32[]{:S(2)}) collective-permute-start(bf16[256,256]{1,0:T(8,128)(2,1)} %get-tuple-element.105.k_in), channel_id=1, source_target_pairs={{0,4},{1,5},{2,6},{3,7},{4,0},{5,1},{6,2},{7,3},{8,12},{9,13},{10,... | collective-permute-start | bytes 393224 | tf_op jit(solution)/shard_map/cond/branch_0_fun/ppermute | solution.py:400
  7.4 0.0 slice-start
  7.4 2.4 %own.2 = (s32[1,256]{1,0:T(1,128)S(1)}, bf16[256,1024]{1,0:T(8,128)(2,1)S(1)}, f32[8,256]{1,0:T(8,128)S(1)}, f32[8,256]{1,0:T(8,128)S(1)}, f32[8,128,256]{2,1,0:T(8,128)S(1)}) custom-call(s32[5]{0:T(128)} %get-tuple-element.29.offsets_in, bf16[256,1024]{1,0:T(8,128)(2,1)} %get-tuple-element.103.q_in, bf16[256,256]{1,0:T(8,128)(2,1)} %get-tuple-element.105.k_in, ...), custom_call_target="tpu_custom_call" | custom-call | flops 1342177280 | tf_op jit(solution)/shard_map/cond/branch_0_fun/own/pallas_call | solution.py:144
  9.9 0.0 collective-permute-done.3.k_ref
  9.9 0.1 collective-permute-start.4
  10.0 0.0 collective-permute-done.v_ref
  10.0 3.0 %collective-permute-start.1 = (bf16[256,256]{1,0:T(8,128)(2,1)S(1)}, bf16[256,256]{1,0:T(8,128)(2,1)S(1)}, u32[]{:S(2)}, u32[]{:S(2)}) collective-permute-start(bf16[256,256]{1,0:T(8,128)(2,1)S(1)} %collective-permute-done.v_ref), channel_id=1, source_target_pairs={{0,8},{1,9},{2,10},{3,11},{4,12},{5,13},{6,14},{7,15},{8,0},{9,1},... | collective-permute-start | bytes 393224 | tf_op jit(solution)/shard_map/cond/branch_0_fun/ppermute | solution.py:400
  13.0 0.0 collective-permute-start.2
  13.0 0.0 collective-permute-done.6.v_ref
  13.0 0.1 attend.6
  13.2 0.0 collective-permute-done.5.k_ref
  13.2 0.0 slice-start.1
  13.2 0.2 attend.7
  13.4 0.0 collective-permute-done.4.k_ref
  13.4 0.1 last_scores.2
  13.5 2.5 %collective-permute-done.1.refs_0_ = bf16[256,256]{1,0:T(8,128)(2,1)S(1)} collective-permute-done((bf16[256,256]{1,0:T(8,128)(2,1)S(1)}, bf16[256,256]{1,0:T(8,128)(2,1)S(1)}, u32[]{:S(2)}, u32[]{:S(2)}) %collective-permute-start.1) | collective-permute-done | bytes 131104 | tf_op jit(solution)/shard_map/cond/branch_0_fun/ppermute | solution.py:400
  16.0 0.0 collective-permute-done.2.refs_1_
  16.0 0.0 slice-done
  16.0 0.0 slice-done.1
  16.0 0.8 %finish.2 = (bf16[256,1024]{1,0:T(8,128)(2,1)S(1)}, bf16[1,256,512]{2,1,0:T(8,128)(2,1)S(1)}) custom-call(bf16[256,256]{1,0:T(8,128)(2,1)S(1)} %collective-permute-done.1.refs_0_, bf16[256,256]{1,0:T(8,128)(2,1)S(1)} %collective-permute-done.2.refs_1_, bf16[8,256,256]{2,1,0:T(8,128)(2,1)S(1)} %get-tuple-element.46.refs_2_, ...), custom_call_target="tpu_custom_call" | custom-call | tf_op jit(solution)/shard_map/cond/branch_0_fun/finish/pallas_call | solution.py:283
  16.8 0.1 collective-permute-start.7
  16.8 1.0 %rest.2 = (bf16[1,256,512]{2,1,0:T(8,128)(2,1)S(1)}, bf16[1,256,1024]{2,1,0:T(8,128)(2,1)S(1)}) custom-call(bf16[256,1024]{1,0:T(8,128)(2,1)S(1)} %get-tuple-element.51.att_ref, bf16[1024,4096]{1,0:T(8,128)(2,1)S(1)} %bitcast.18), custom_call_target="tpu_custom_call" | custom-call | flops 805306368 | tf_op jit(solution)/shard_map/cond/branch_0_fun/rest/pallas_call | solution.py:306
  17.9 0.5 %collective-permute-done.7.refs_0_ = bf16[1,256,512]{2,1,0:T(8,128)(2,1)S(1)} collective-permute-done((bf16[1,256,512]{2,1,0:T(8,128)(2,1)S(1)}, bf16[1,256,512]{2,1,0:T(8,128)(2,1)S(1)}, u32[]{:S(2)}, u32[]{:S(2)}) %collective-permute-start.7) | collective-permute-done | bytes 262176 | tf_op jit(solution)/shard_map/cond/branch_0_fun/ppermute | solution.py:360
  18.4 0.5 %sent.4 = bf16[1,256,512]{2,1,0:T(8,128)(2,1)S(1)} custom-call(bf16[256,1024]{1,0:T(8,128)(2,1)S(1)} %get-tuple-element.51.att_ref, bf16[1024,4096]{1,0:T(8,128)(2,1)S(1)} %bitcast.18, bf16[1,256,512]{2,1,0:T(8,128)(2,1)S(1)} %collective-permute-done.7.refs_0_), custom_call_target="tpu_custom_call" | custom-call | flops 268435456 | tf_op jit(solution)/shard_map/cond/branch_0_fun/sent/pallas_call | solution.py:325
  18.8 0.2 collective-permute-start.8
  19.0 0.4 %collective-permute-start.9 = (bf16[1,256,512]{2,1,0:T(8,128)(2,1)S(1)}, bf16[1,256,512]{2,1,0:T(8,128)(2,1)S(1)}, u32[]{:S(2)}, u32[]{:S(2)}) collective-permute-start(bf16[1,256,512]{2,1,0:T(8,128)(2,1)S(1)} %get-tuple-element.55), channel_id=1, source_target_pairs={{0,1},{1,0},{2,3},{3,2},{4,5},{5,4},{6,7},{7,6},{8,9},{9,8},{10,11... | collective-permute-start | bytes 786440 | tf_op jit(solution)/shard_map/cond/branch_0_fun/ppermute | solution.py:360
  19.4 1.5 %collective-permute-start.11 = (bf16[1,256,512]{2,1,0:T(8,128)(2,1)S(1)}, bf16[1,256,512]{2,1,0:T(8,128)(2,1)S(1)}, u32[]{:S(2)}, u32[]{:S(2)}) collective-permute-start(bf16[1,256,512]{2,1,0:T(8,128)(2,1)S(1)} %sent.4), channel_id=1, source_target_pairs={{0,2},{1,3},{2,0},{3,1},{4,6},{5,7},{6,4},{7,5},{8,10},{9,11},{10,... | collective-permute-start | bytes 786440 | tf_op jit(solution)/shard_map/cond/branch_0_fun/ppermute | solution.py:360
  20.9 0.3 collective-permute-done.9.refs_0_
  21.2 0.5 %sent.5 = bf16[1,256,512]{2,1,0:T(8,128)(2,1)S(1)} custom-call(bf16[256,1024]{1,0:T(8,128)(2,1)S(1)} %get-tuple-element.51.att_ref, bf16[1024,4096]{1,0:T(8,128)(2,1)S(1)} %bitcast.18, bf16[1,256,512]{2,1,0:T(8,128)(2,1)S(1)} %collective-permute-done.9.refs_0_), custom_call_target="tpu_custom_call" | custom-call | flops 268435456 | tf_op jit(solution)/shard_map/cond/branch_0_fun/sent/pallas_call | solution.py:325
  21.7 1.6 %collective-permute-start.10 = (bf16[1,256,512]{2,1,0:T(8,128)(2,1)S(1)}, bf16[1,256,512]{2,1,0:T(8,128)(2,1)S(1)}, u32[]{:S(2)}, u32[]{:S(2)}) collective-permute-start(bf16[1,256,512]{2,1,0:T(8,128)(2,1)S(1)} %sent.5), channel_id=1, source_target_pairs={{0,2},{1,3},{2,0},{3,1},{4,6},{5,7},{6,4},{7,5},{8,10},{9,11},{10,... | collective-permute-start | bytes 786440 | tf_op jit(solution)/shard_map/cond/branch_0_fun/ppermute | solution.py:360
  23.3 0.0 collective-permute-done.8.refs_0_
  23.3 0.5 %kept.5 = f32[1,256,512]{2,1,0:T(8,128)S(1)} custom-call(bf16[256,1024]{1,0:T(8,128)(2,1)S(1)} %get-tuple-element.51.att_ref, bf16[1024,4096]{1,0:T(8,128)(2,1)S(1)} %bitcast.18, bf16[1,256,1024]{2,1,0:T(8,128)(2,1)S(1)} %collective-permute-done.8.refs_0_), custom_call_target="tpu_custom_call" | custom-call | flops 268435456 | tf_op jit(solution)/shard_map/cond/branch_0_fun/kept/pallas_call | solution.py:325
  23.7 4.8 %collective-permute-done.11 = bf16[1,256,512]{2,1,0:T(8,128)(2,1)S(1)} collective-permute-done((bf16[1,256,512]{2,1,0:T(8,128)(2,1)S(1)}, bf16[1,256,512]{2,1,0:T(8,128)(2,1)S(1)}, u32[]{:S(2)}, u32[]{:S(2)}) %collective-permute-start.11) | collective-permute-done | bytes 262176 | tf_op jit(solution)/shard_map/cond/branch_0_fun/ppermute | solution.py:360
  28.6 0.8 %output.4.refs_0_ = bf16[1024,256]{1,0:T(8,128)(2,1)} custom-call(f32[256,512]{1,0:T(8,128)S(1)} %bitcast.11, bf16[256,512]{1,0:T(8,128)(2,1)S(1)} %bitcast.13), custom_call_target="tpu_custom_call" | custom-call | tf_op jit(solution)/shard_map/cond/branch_0_fun/output/pallas_call | solution.py:347
  29.4 0.5 %kept.4 = f32[1,256,512]{2,1,0:T(8,128)S(1)} custom-call(bf16[256,1024]{1,0:T(8,128)(2,1)S(1)} %get-tuple-element.51.att_ref, bf16[1024,4096]{1,0:T(8,128)(2,1)S(1)} %bitcast.18, bf16[1,256,1024]{2,1,0:T(8,128)(2,1)S(1)} %collective-permute-done.8.refs_0_), custom_call_target="tpu_custom_call" | custom-call | flops 268435456 | tf_op jit(solution)/shard_map/cond/branch_0_fun/kept/pallas_call | solution.py:325
  29.9 3.5 %collective-permute-done.10 = bf16[1,256,512]{2,1,0:T(8,128)(2,1)S(1)} collective-permute-done((bf16[1,256,512]{2,1,0:T(8,128)(2,1)S(1)}, bf16[1,256,512]{2,1,0:T(8,128)(2,1)S(1)}, u32[]{:S(2)}, u32[]{:S(2)}) %collective-permute-start.10) | collective-permute-done | bytes 262176 | tf_op jit(solution)/shard_map/cond/branch_0_fun/ppermute | solution.py:360
  33.4 0.8 %output.5 = bf16[1024,256]{1,0:T(8,128)(2,1)} custom-call(f32[256,512]{1,0:T(8,128)S(1)} %bitcast.9, bf16[256,512]{1,0:T(8,128)(2,1)S(1)} %bitcast.14, bf16[1024,256]{1,0:T(8,128)(2,1)} %output.4.refs_0_), custom_call_target="tpu_custom_call", output_to_operand_aliasing={{}: (2, {})} | custom-call | tf_op jit(solution)/shard_map/cond/branch_0_fun/output/pallas_call | solution.py:347
  (1 shorter events, 0.0 us)
Async XLA Ops:
  0.7 9.1 %collective-permute-start.3 = (bf16[256,256]{1,0:T(8,128)(2,1)}, bf16[256,256]{1,0:T(8,128)(2,1)S(1)}, u32[]{:S(2)}, u32[]{:S(2)}) collective-permute-start(bf16[256,256]{1,0:T(8,128)(2,1)} %get-tuple-element.105.k_in), channel_id=1, source_target_pairs={{0,8},{1,9},{2,10},{3,11},{4,12},{5,13},{6,14},{7,15},{8,16},{9,17... | collective-permute-start | bytes 393224 | tf_op jit(solution)/shard_map/cond/branch_0_fun/ppermute | solution.py:400
  3.8 6.2 %collective-permute-start = (bf16[256,256]{1,0:T(8,128)(2,1)}, bf16[256,256]{1,0:T(8,128)(2,1)S(1)}, u32[]{:S(2)}, u32[]{:S(2)}) collective-permute-start(bf16[256,256]{1,0:T(8,128)(2,1)} %get-tuple-element.101.v_in), channel_id=1, source_target_pairs={{0,4},{1,5},{2,6},{3,7},{4,0},{5,1},{6,2},{7,3},{8,12},{9,13},{10,... | collective-permute-start | bytes 393224 | tf_op jit(solution)/shard_map/cond/branch_0_fun/ppermute | solution.py:400
  5.3 7.7 %collective-permute-start.6 = (bf16[256,256]{1,0:T(8,128)(2,1)}, bf16[256,256]{1,0:T(8,128)(2,1)S(1)}, u32[]{:S(2)}, u32[]{:S(2)}) collective-permute-start(bf16[256,256]{1,0:T(8,128)(2,1)} %get-tuple-element.101.v_in), channel_id=1, source_target_pairs={{0,8},{1,9},{2,10},{3,11},{4,12},{5,13},{6,14},{7,15},{8,16},{9,17... | collective-permute-start | bytes 393224 | tf_op jit(solution)/shard_map/cond/branch_0_fun/ppermute | solution.py:400
  6.9 6.3 %collective-permute-start.5 = (bf16[256,256]{1,0:T(8,128)(2,1)}, bf16[256,256]{1,0:T(8,128)(2,1)S(1)}, u32[]{:S(2)}, u32[]{:S(2)}) collective-permute-start(bf16[256,256]{1,0:T(8,128)(2,1)} %get-tuple-element.105.k_in), channel_id=1, source_target_pairs={{0,4},{1,5},{2,6},{3,7},{4,0},{5,1},{6,2},{7,3},{8,12},{9,13},{10,... | collective-permute-start | bytes 393224 | tf_op jit(solution)/shard_map/cond/branch_0_fun/ppermute | solution.py:400
  7.4 8.5 %slice-start = ((s8[8388608]{0:T(1024)(128)(4,1)}), s8[4194304]{0:T(1024)(128)(4,1)S(1)}, s32[]{:S(2)}) async-start(s8[8388608]{0:T(1024)(128)(4,1)} %bitcast.17), calls=%async_computation | async-start | bytes 8388608 | tf_op jit(solution)/shard_map/cond
  9.9 3.5 %collective-permute-start.4 = (bf16[256,256]{1,0:T(8,128)(2,1)S(1)}, bf16[256,256]{1,0:T(8,128)(2,1)S(1)}, u32[]{:S(2)}, u32[]{:S(2)}) collective-permute-start(bf16[256,256]{1,0:T(8,128)(2,1)S(1)} %collective-permute-done.3.k_ref), channel_id=1, source_target_pairs={{0,1},{1,0},{2,3},{3,2},{4,5},{5,4},{6,7},{7,6},{8,12},{9,13},{10,... | collective-permute-start | bytes 393224 | tf_op jit(solution)/shard_map/cond/branch_0_fun/ppermute | solution.py:400
  10.0 6.0 %collective-permute-start.1 = (bf16[256,256]{1,0:T(8,128)(2,1)S(1)}, bf16[256,256]{1,0:T(8,128)(2,1)S(1)}, u32[]{:S(2)}, u32[]{:S(2)}) collective-permute-start(bf16[256,256]{1,0:T(8,128)(2,1)S(1)} %collective-permute-done.v_ref), channel_id=1, source_target_pairs={{0,8},{1,9},{2,10},{3,11},{4,12},{5,13},{6,14},{7,15},{8,0},{9,1},... | collective-permute-start | bytes 393224 | tf_op jit(solution)/shard_map/cond/branch_0_fun/ppermute | solution.py:400
  13.0 2.9 %collective-permute-start.2 = (bf16[256,256]{1,0:T(8,128)(2,1)S(1)}, bf16[256,256]{1,0:T(8,128)(2,1)S(1)}, u32[]{:S(2)}, u32[]{:S(2)}) collective-permute-start(bf16[256,256]{1,0:T(8,128)(2,1)S(1)} %collective-permute-done.v_ref), channel_id=1, source_target_pairs={{0,1},{1,0},{2,3},{3,2},{4,5},{5,4},{6,7},{7,6},{8,16},{9,17},{10,... | collective-permute-start | bytes 393224 | tf_op jit(solution)/shard_map/cond/branch_0_fun/ppermute | solution.py:400
  13.2 2.8 %slice-start.1 = ((s8[8388608]{0:T(1024)(128)(4,1)}), s8[4194304]{0:T(1024)(128)(4,1)S(1)}, s32[]{:S(2)}) async-start(s8[8388608]{0:T(1024)(128)(4,1)} %bitcast.17), calls=%async_computation.1 | async-start | bytes 8388608 | tf_op jit(solution)/shard_map/cond
  16.8 1.6 %collective-permute-start.7 = (bf16[1,256,512]{2,1,0:T(8,128)(2,1)S(1)}, bf16[1,256,512]{2,1,0:T(8,128)(2,1)S(1)}, u32[]{:S(2)}, u32[]{:S(2)}) collective-permute-start(bf16[1,256,512]{2,1,0:T(8,128)(2,1)S(1)} %get-tuple-element.53), channel_id=1, source_target_pairs={{0,1},{1,0},{2,3},{3,2},{4,5},{5,4},{6,7},{7,6},{8,9},{9,8},{10,11... | collective-permute-start | bytes 786440 | tf_op jit(solution)/shard_map/cond/branch_0_fun/ppermute | solution.py:360
  18.8 4.4 %collective-permute-start.8 = (bf16[1,256,1024]{2,1,0:T(8,128)(2,1)S(1)}, bf16[1,256,1024]{2,1,0:T(8,128)(2,1)S(1)}, u32[]{:S(2)}, u32[]{:S(2)}) collective-permute-start(bf16[1,256,1024]{2,1,0:T(8,128)(2,1)S(1)} %get-tuple-element.54), channel_id=1, source_target_pairs={{0,1},{1,0},{2,3},{3,2},{4,5},{5,4},{6,7},{7,6},{8,9},{9,8},{10,11... | collective-permute-start | bytes 1572872 | tf_op jit(solution)/shard_map/cond/branch_0_fun/ppermute | solution.py:360
  19.0 2.1 %collective-permute-start.9 = (bf16[1,256,512]{2,1,0:T(8,128)(2,1)S(1)}, bf16[1,256,512]{2,1,0:T(8,128)(2,1)S(1)}, u32[]{:S(2)}, u32[]{:S(2)}) collective-permute-start(bf16[1,256,512]{2,1,0:T(8,128)(2,1)S(1)} %get-tuple-element.55), channel_id=1, source_target_pairs={{0,1},{1,0},{2,3},{3,2},{4,5},{5,4},{6,7},{7,6},{8,9},{9,8},{10,11... | collective-permute-start | bytes 786440 | tf_op jit(solution)/shard_map/cond/branch_0_fun/ppermute | solution.py:360
  19.4 9.2 %collective-permute-start.11 = (bf16[1,256,512]{2,1,0:T(8,128)(2,1)S(1)}, bf16[1,256,512]{2,1,0:T(8,128)(2,1)S(1)}, u32[]{:S(2)}, u32[]{:S(2)}) collective-permute-start(bf16[1,256,512]{2,1,0:T(8,128)(2,1)S(1)} %sent.4), channel_id=1, source_target_pairs={{0,2},{1,3},{2,0},{3,1},{4,6},{5,7},{6,4},{7,5},{8,10},{9,11},{10,... | collective-permute-start | bytes 786440 | tf_op jit(solution)/shard_map/cond/branch_0_fun/ppermute | solution.py:360
  21.7 11.7 %collective-permute-start.10 = (bf16[1,256,512]{2,1,0:T(8,128)(2,1)S(1)}, bf16[1,256,512]{2,1,0:T(8,128)(2,1)S(1)}, u32[]{:S(2)}, u32[]{:S(2)}) collective-permute-start(bf16[1,256,512]{2,1,0:T(8,128)(2,1)S(1)} %sent.5), channel_id=1, source_target_pairs={{0,2},{1,3},{2,0},{3,1},{4,6},{5,7},{6,4},{7,5},{8,10},{9,11},{10,... | collective-permute-start | bytes 786440 | tf_op jit(solution)/shard_map/cond/branch_0_fun/ppermute | solution.py:360
